TPU v7x, 32 devices: a whole 2x2x4 slice. The times are simulated.
32 devices in a mesh: dp: 4 (over y, x), ctx: 8 (over z, core).
Axes of the slice: x: 2, y: 2, z: 4, core: 2. Of those that a mesh axis runs over, the one named last changes fastest.
Arguments:
- phonemes: bfloat16 [4, 1024, 1024], P('dp', 'ctx'), may hold values from -6 to 6
- conv_kernel: float32 [7, 1024], replicated, may hold values from -2 to 2
- enc_gain: float32 [1024], replicated, may hold values from 0.1 to 1.9
- enc_in_weight: bfloat16 [1024, 1024], replicated, may hold values from -0.1875 to 0.1875
- enc_out_weight: bfloat16 [1024, 1024], replicated, may hold values from -0.1875 to 0.1875
- proj_weight: bfloat16 [1024, 1536], replicated, may hold values from -0.1875 to 0.1875
- hidden: bfloat16 [4, 4096, 1536], P('dp', 'ctx'), may hold values from -6 to 6
- durations: int32 [4, 1024], P('dp'), may hold values from 1 to 13, as said below
- utt_counts: int32 [4, 4], P('dp'), may hold values from 1 to 512, 1024 in all within a row
- timesteps: int32 [4, 4], P('dp'), may hold values from 0 to 999
- ada_weight: bfloat16 [256, 4608], replicated, may hold values from -0.375 to 0.375
- ff_in_weight: bfloat16 [1536, 2048], replicated, may hold values from -0.15625 to 0.15625
- ff_out_weight: bfloat16 [2048, 1536], replicated, may hold values from -0.125 to 0.125
- cotangent: bfloat16 [4, 4096, 1536], P('dp', 'ctx'), may hold values from -6 to 6
Outputs:
- transformer_layer_output: bfloat16 [4, 4096, 1536], P('dp', 'ctx')
- d_hidden: bfloat16 [4, 4096, 1536], P('dp', 'ctx')
- encoder_output_gradient: bfloat16 [4, 1024, 1024], P('dp', 'ctx')
- projection_weight_gradient: float32 [1024, 1536], P(('dp', 'ctx'))
Inputs may be any that keep to these rules, and one draw needn't show every extreme that they name: In every replica the durations sum to 4096; the frames of the device at ctx index i are covered by phonemes i * 128 - 2 through (i + 1) * 128 + 1, and in every replica some device needs all 2 rows below its phonemes and some device all 2 rows above them; one duration is exactly 13. `utt_counts`: in every replica the counts sum to 1024 and one is exactly 512.
All inputs are finite; a program needn't handle non-finite values.
Results may differ from a plain program's by a relative error of at most 0.015.
Values may be sent and summed in bfloat16 or wider, within the bound.
A program may use at most 128 MiB of HBM per device.

v0:
```python
import math

import jax
import jax.numpy as jnp
from jax import lax
from jax.sharding import PartitionSpec as P

RIM = 2


tanh_scale = 0.7978845608028654


def extended_2(value, sides, width):
    for axis, dim in sides:
        size, length = (lax.axis_size(axis), value.shape[dim])
        up = [(i, (i + 1) % size) for i in range(size - 1)]
        down = [(j, i) for i, j in up]
        last = lax.slice_in_dim(value, length - width, length, axis=dim)
        initial = lax.slice_in_dim(value, 0, width, axis=dim)
        before = lax.ppermute(last, axis, up)
        after = lax.ppermute(initial, axis, down)
        value = jnp.concatenate([before, value, after], axis=dim)
    return value


def shifted(value, axis, by):
    length = lax.axis_size(axis)
    pairs = [(i, i + by) for i in range(length) if 0 <= i + by < length]
    return lax.ppermute(value, axis, pairs)


def gelu_value(inputs):
    inner = tanh_scale * (inputs + 0.044715 * inputs * inputs * inputs)
    return 0.5 * inputs * (1.0 + jnp.tanh(inner))


def gelu_slope(inputs):
    squared = inputs * inputs
    hyper = jnp.tanh(tanh_scale * (inputs + 0.044715 * squared * inputs))
    return 0.5 * (1.0 + hyper) + 0.5 * inputs * (1.0 - hyper * hyper) * tanh_scale * (
        1.0 + 3.0 * 0.044715 * squared
    )


def time_embed(timestep_ids, width):
    half_width = width // 2
    frequency = jnp.exp(-math.log(10000.0) * jnp.arange(half_width, dtype=jnp.float32) / half_width)
    angles = timestep_ids.astype(jnp.float32)[:, None] * frequency[None, :]
    return jnp.concatenate([jnp.sin(angles), jnp.cos(angles)], axis=1)


def rms_scale(values):
    return lax.rsqrt(jnp.mean(values * values, axis=-1, keepdims=True) + 1e-06)


def split_parts(values):
    upper_part = lax.optimization_barrier(values.astype(jnp.bfloat16))
    lower_part = (values - upper_part.astype(jnp.float32)).astype(jnp.bfloat16)
    return (upper_part, lower_part)


def contract_rows(left, right):
    return lax.dot_general(
        left, right, (((0,), (0,)), ((), ())), preferred_element_type=jnp.float32
    )


def contract_cols(left, right):
    return lax.dot_general(
        left, right, (((1,), (1,)), ((), ())), preferred_element_type=jnp.float32
    )


def fold_edges(window_sums, phone_local, from_lower, from_upper):
    own_rows = window_sums[RIM : RIM + phone_local]
    lower_rows = own_rows[:RIM] + from_lower
    middle_rows = own_rows[RIM : phone_local - RIM]
    upper_rows = own_rows[phone_local - RIM :] + from_upper
    return jnp.concatenate([lower_rows, middle_rows, upper_rows], axis=0)


def shards(
    phonemes,
    conv_kernel,
    enc_gain,
    enc_in_weight,
    enc_out_weight,
    proj_weight,
    hidden,
    durations,
    utt_counts,
    timesteps,
    ada_weight,
    ff_in_weight,
    ff_out_weight,
    cotangent,
):
    ctx_index = lax.axis_index("ctx")
    ctx_count = lax.axis_size("ctx")
    dp_count = lax.axis_size("dp")
    phone_rows = phonemes[0]
    phone_local = phone_rows.shape[0]
    frame_local = hidden.shape[1]
    model_width = hidden.shape[2]
    utt_ends = jnp.cumsum(utt_counts[0])
    extended = extended_2(phone_rows, (("ctx", 0),), 3)
    positions = ctx_index * phone_local - 3 + jnp.arange(phone_local + 6, dtype=jnp.int32)
    segment = jnp.sum((utt_ends[None, :] <= positions[:, None]).astype(jnp.int32), axis=1)
    centre = segment[3 : 3 + phone_local]
    mixed = jnp.zeros((phone_local, phone_rows.shape[1]), jnp.float32)
    for offset in range(7):
        same_utt = (segment[offset : offset + phone_local] == centre).astype(jnp.float32)
        mixed = (
            mixed
            + conv_kernel[offset][None, :]
            * extended[offset : offset + phone_local].astype(jnp.float32)
            * same_utt[:, None]
        )
    normed = (mixed * rms_scale(mixed) * enc_gain[None, :]).astype(jnp.bfloat16)
    inner = gelu_value(jnp.dot(normed, enc_in_weight, preferred_element_type=jnp.float32)).astype(
        jnp.bfloat16
    )
    encoded = (
        phone_rows.astype(jnp.float32)
        + jnp.dot(inner, enc_out_weight, preferred_element_type=jnp.float32)
    ).astype(jnp.bfloat16)
    phone_dur = durations[0]
    phone_end = jnp.cumsum(phone_dur)
    phone_begin = phone_end - phone_dur
    frame_ids = ctx_index * frame_local + jnp.arange(frame_local, dtype=jnp.int32)
    window_rows = phone_local + 2 * RIM
    begin_padded = jnp.pad(phone_begin, RIM, constant_values=-1)
    end_padded = jnp.pad(phone_end, RIM, constant_values=-1)
    begin_window = lax.dynamic_slice_in_dim(begin_padded, ctx_index * phone_local, window_rows)
    end_window = lax.dynamic_slice_in_dim(end_padded, ctx_index * phone_local, window_rows)
    onehot = (
        (frame_ids[:, None] >= begin_window[None, :]) & (frame_ids[:, None] < end_window[None, :])
    ).astype(jnp.bfloat16)
    cond = jnp.dot(encoded, proj_weight, preferred_element_type=jnp.float32).astype(jnp.bfloat16)
    cond_window = extended_2(cond, (("ctx", 0),), RIM)
    cond_frames = jnp.dot(onehot, cond_window, preferred_element_type=jnp.float32).astype(
        jnp.bfloat16
    )
    utt_marks = (
        jnp.arange(phone_dur.shape[0], dtype=jnp.int32)[None, :] < utt_ends[:, None]
    ).astype(jnp.int32)
    utt_frame_end = jnp.sum(utt_marks * phone_dur[None, :], axis=1)
    utt_frame_begin = jnp.concatenate([jnp.zeros((1,), jnp.int32), utt_frame_end[:-1]])
    utt_onehot = (
        (frame_ids[:, None] >= utt_frame_begin[None, :])
        & (frame_ids[:, None] < utt_frame_end[None, :])
    ).astype(jnp.float32)
    act = jax.nn.silu(time_embed(timesteps[0], ada_weight.shape[0])).astype(jnp.bfloat16)
    modul = jnp.dot(act, ada_weight, preferred_element_type=jnp.float32)
    frame_mod = jnp.dot(utt_onehot, modul, precision=lax.Precision.HIGHEST)
    shift = frame_mod[:, :model_width]
    scale = frame_mod[:, model_width : 2 * model_width]
    gate_values = frame_mod[:, 2 * model_width :]
    residual_stream = hidden[0].astype(jnp.float32) + cond_frames.astype(jnp.float32)
    rinv = rms_scale(residual_stream)
    normed2 = (residual_stream * rinv * (1.0 + scale) + shift).astype(jnp.bfloat16)
    pre = jnp.dot(normed2, ff_in_weight, preferred_element_type=jnp.float32)
    hidact = gelu_value(pre).astype(jnp.bfloat16)
    perceptron_output = jnp.dot(hidact, ff_out_weight, preferred_element_type=jnp.float32)
    transformer_layer_output = (residual_stream + gate_values * perceptron_output).astype(
        jnp.bfloat16
    )
    cot = cotangent[0].astype(jnp.float32)
    d_mlp = (gate_values * cot).astype(jnp.bfloat16)
    d_act = contract_cols(d_mlp, ff_out_weight)
    d_pre = (d_act * gelu_slope(pre)).astype(jnp.bfloat16)
    d_norm = contract_cols(d_pre, ff_in_weight)
    d_hat = d_norm * (1.0 + scale)
    d_resid = (
        cot
        + rinv * d_hat
        - residual_stream
        * rinv
        * rinv
        * rinv
        * jnp.mean(d_hat * residual_stream, axis=-1, keepdims=True)
    )
    frame_gradient_rows = d_resid.astype(jnp.bfloat16)
    window_sums = contract_rows(onehot, frame_gradient_rows)
    from_lower = shifted(window_sums[RIM + phone_local :], "ctx", 1)
    from_upper = shifted(window_sums[:RIM], "ctx", -1)
    d_cond = fold_edges(window_sums, phone_local, from_lower, from_upper)
    cond_upper, cond_lower = split_parts(d_cond)
    encoder_output_gradient = (
        contract_cols(cond_upper, proj_weight) + contract_cols(cond_lower, proj_weight)
    ).astype(jnp.bfloat16)
    proj_term = contract_rows(encoded, cond_upper) + contract_rows(encoded, cond_lower)
    norm_factor = 1.0 / math.sqrt(dp_count * ctx_count * frame_local)
    replica_rows = lax.psum_scatter(
        proj_term.astype(jnp.bfloat16), "dp", scatter_dimension=0, tiled=True
    )
    grad_total = lax.psum_scatter(replica_rows, "ctx", scatter_dimension=0, tiled=True).astype(
        jnp.float32
    )
    projection_weight_gradient = grad_total * norm_factor
    return (
        transformer_layer_output[None],
        frame_gradient_rows[None],
        encoder_output_gradient[None],
        projection_weight_gradient,
    )


def solution(mesh):
    in_specs = (
        P("dp", "ctx", None),
        P(),
        P(),
        P(),
        P(),
        P(),
        P("dp", "ctx", None),
        P("dp", None),
        P("dp", None),
        P("dp", None),
        P(),
        P(),
        P(),
        P("dp", "ctx", None),
    )
    out_specs = (
        P("dp", "ctx", None),
        P("dp", "ctx", None),
        P("dp", "ctx", None),
        P(("dp", "ctx"), None),
    )
    return jax.shard_map(shards, mesh=mesh, in_specs=in_specs, out_specs=out_specs, check_vma=False)
```

profile of v0, /device:TPU:0, one launch (start us, length us, event | category | flops | bytes accessed | tf_op | source)
XLA Modules:
  0.0 176.6 jit_solution(7280162598817453353)
XLA Ops:
  7.2 0.0 reduce-scatter.3.cloned.1.call-start
  7.2 0.9 slice_bitcast_fusion.1
  8.1 2.5 %collective-permute-start = (bf16[3,1024]{1,0:T(4,128)(2,1)S(1)}, bf16[3,1024]{1,0:T(4,128)(2,1)S(1)}, u32[]{:S(2)}, u32[]{:S(2)}) collective-permute-start(bf16[3,1024]{1,0:T(4,128)(2,1)S(1)} %get-tuple-element.12), channel_id=1, source_target_pairs={{0,1},{1,2},{2,3},{3,4},{4,5},{5,6},{6,7},{8,9},{9,10},{10,11},{11... | collective-permute-start | bytes 18440 | tf_op jit(solution)/shard_map/ppermute | solution.py:21
  10.6 1.3 collective-permute-start.1
  11.9 0.7 convert_bitcast_fusion
  12.6 0.8 reduce-window.21
  13.4 0.9 select_reduce_fusion
  14.3 0.1 convert_reduce_fusion
  14.4 1.0 reduce-window.19
  15.4 0.1 slice.123
  15.5 0.1 slice_reduce_fusion
  15.6 0.8 fusion.93
  16.4 1.0 fusion.96
  17.4 0.1 pad_add_fusion
  17.5 0.1 multiply_sine_fusion
  17.6 2.1 %fusion.73 = f32[4,4608]{1,0:T(4,128)S(1)} fusion(bf16[256,4608]{1,0:T(8,128)(2,1)} %param.24, f32[4,128]{1,0:T(4,128)S(1)} %get-tuple-element.22, f32[4,128]{1,0:T(4,128)S(1)} %get-tuple-element.21), kind=kOutput, calls=%fused_computation.112 | convolution fusion | flops 9443328 | bytes 2437120 | tf_op jit(solution)/shard_map/dot_general | solution.py:155
  19.7 6.5 %fusion.65 = f32[512,4608]{1,0:T(8,128)} fusion(f32[4,4608]{1,0:T(4,128)S(1)} %fusion.73, s32[512]{0:T(512)S(1)} %iota_add_fusion, s32[4]{0:T(128)S(1)} %select_reduce_fusion, s32[4]{0:T(128)S(1)} %pad_add_fusion), kind=kOutput, calls=%fused_computation.97 | convolution fusion | flops 113252352 | bytes 9512992 | tf_op jit(solution)/shard_map/dot_general | solution.py:156
  26.2 0.1 compare_convert_fusion.5
  26.3 1.6 multiply_reduce_fusion.2
  27.9 3.3 %fusion.28 = bf16[128,1024]{1,0:T(8,128)(2,1)S(1)} fusion(bf16[1024,1024]{1,0:T(8,128)(2,1)} %param.18, bf16[1024,1024]{1,0:T(8,128)(2,1)} %param.17, f32[128,1024]{1,0:T(8,128)} %get-tuple-element.7, f32[1024]{0:T(1024)S(1)} %copy-done.9, f32[128]{0:T(128)S(1)} %add_rsqrt_fusion.1, bf16[1,128,1024]{2,1,0:T(8,128)(2,1)} %param.14), kind=kOutput, calls=%fused_computation.40 | convolution fusion | flops 538836992 | bytes 5247488 | tf_op jit(solution)/shard_map/dot_general | solution.py:126
  31.2 0.6 convolution_convert_fusion.1
  31.8 5.2 %collective-permute-start.2 = (bf16[2,1536]{1,0:T(2,128)(2,1)S(1)}, bf16[2,1536]{1,0:T(2,128)(2,1)S(1)}, u32[]{:S(2)}, u32[]{:S(2)}) collective-permute-start(bf16[2,1536]{1,0:T(2,128)(2,1)S(1)} %get-tuple-element.10), channel_id=1, source_target_pairs={{0,1},{1,2},{2,3},{3,4},{4,5},{5,6},{6,7},{8,9},{9,10},{10,11},{11... | collective-permute-start | bytes 18440 | tf_op jit(solution)/shard_map/ppermute | solution.py:21
  37.0 1.5 collective-permute-start.3
  38.5 0.1 pad_dynamic-slice_fusion
  38.6 2.7 %collective-permute-done.3 = bf16[2,1536]{1,0:T(2,128)(2,1)S(1)} collective-permute-done((bf16[2,1536]{1,0:T(2,128)(2,1)S(1)}, bf16[2,1536]{1,0:T(2,128)(2,1)S(1)}, u32[]{:S(2)}, u32[]{:S(2)}) %collective-permute-start.3) | collective-permute-done | bytes 6176 | tf_op jit(solution)/shard_map/ppermute | solution.py:22
  41.3 0.8 multiply_reduce_fusion.1
  42.2 1.6 copy-done.1
  43.8 10.2 %fusion.19 = f32[512,2048]{1,0:T(8,128)} fusion(bf16[1536,2048]{1,0:T(8,128)(2,1)} %param.25, f32[512,4608]{1,0:T(8,128)} %fusion.65, f32[512,1536]{1,0:T(8,128)S(1)} %get-tuple-element.30, f32[512]{0:T(512)S(1)} %add_rsqrt_fusion), kind=kOutput, calls=%fused_computation.33 | convolution fusion | flops 3225157632 | bytes 19924992 | tf_op jit(solution)/shard_map/dot_general | solution.py:163
  54.0 16.8 %multiply_reduce_fusion = (f32[512]{0:T(512)S(1)}, f32[512,1536]{1,0:T(8,128)}) fusion(f32[512,1536]{1,0:T(8,128)} %copy-done.1, f32[512,4608]{1,0:T(8,128)} %fusion.65, bf16[1536,2048]{1,0:T(8,128)(2,1)} %param.25, f32[512,2048]{1,0:T(8,128)} %fusion.19, bf16[2048,1536]{1,0:T(8,128)(2,1)} %param.26, bf16[1,512,1536]{2,1,0:T(8,128)(2,1)} %param.27), kind=kOutput, calls=%fused_computation.23 | convolution fusion | flops 6466829824 | bytes 30935040 | tf_op jit(solution)/shard_map/dot_general | solution.py:70
  70.8 4.2 %fusion.10 = bf16[512,1536]{1,0:T(8,128)(2,1)S(1)} fusion(f32[512,1536]{1,0:T(8,128)} %get-tuple-element.32, f32[512,1536]{1,0:T(8,128)} %copy-done.1, bf16[1,512,1536]{2,1,0:T(8,128)(2,1)} %param.27, f32[512]{0:T(512)S(1)} %broadcast_multiply_fusion, f32[512]{0:T(512)S(1)} %add_rsqrt_fusion), kind=kLoop, calls=%fused_computation.18 | loop fusion | flops 7077888 | bytes 9441280 | tf_op jit(solution)/shard_map/convert_element_type | solution.py:184
  75.0 0.6 fusion.45
  75.6 4.3 %collective-permute-start.4 = (f32[2,1536]{1,0:T(2,128)S(1)}, f32[2,1536]{1,0:T(2,128)S(1)}, u32[]{:S(2)}, u32[]{:S(2)}) collective-permute-start(f32[2,1536]{1,0:T(2,128)S(1)} %slice.175), channel_id=1, source_target_pairs={{0,1},{1,2},{2,3},{3,4},{4,5},{5,6},{6,7},{8,9},{9,10},{10,11},{11... | collective-permute-start | bytes 36872 | tf_op jit(solution)/shard_map/ppermute | solution.py:30
  79.9 0.8 collective-permute-done.4
  80.8 1.3 collective-permute-start.5
  82.1 0.1 slice.176
  82.1 1.7 collective-permute-done.5
  83.8 0.1 fusion.30
  83.9 0.1 subtract_convert_fusion
  84.1 1.0 fusion.100
  85.1 2.7 %add_convert_fusion = bf16[1024,1536]{1,0:T(8,128)(2,1)} fusion(f32[1024,1536]{1,0:T(8,128)S(1)} %fusion.100, bf16[128,1024]{1,0:T(8,128)(2,1)S(1)} %copy-done.4, bf16[128,1536]{1,0:T(8,128)(2,1)S(1)} %subtract_convert_fusion), kind=kOutput, calls=%fused_computation | convolution fusion | flops 405798912 | bytes 10092544 | tf_op jit(solution)/shard_map/dot_general | solution.py:64
  87.8 0.3 reduce-scatter.5.cloned.1.call-start
  88.1 46.3 %reduce-scatter.3.cloned.1.call-done = bf16[256,1536]{1,0:T(8,128)(2,1)} async-done(((bf16[1024,1536]{1,0:T(8,128)(2,1)}), bf16[256,1536]{1,0:T(8,128)(2,1)}) %reduce-scatter.3.cloned.1.call-update) | async-done | bytes 786448 | tf_op jit(solution)/shard_map/reduce_scatter | solution.py:195
  134.4 0.0 reduce-scatter.5.cloned.1.call-update
  134.4 10.7 %fusion.13 = bf16[1,512,1536]{2,1,0:T(8,128)(2,1)} fusion(f32[512,1536]{1,0:T(8,128)} %copy-done.1, bf16[2048,1536]{1,0:T(8,128)(2,1)} %param.26, f32[512,4608]{1,0:T(8,128)} %fusion.65, f32[512,2048]{1,0:T(8,128)} %fusion.19), kind=kOutput, calls=%fused_computation.27 | convolution fusion | flops 3233021952 | bytes 18350080 | tf_op jit(solution)/shard_map/dot_general | solution.py:165
  145.0 1.1 fusion.99
  146.2 1.9 %fusion.29 = bf16[1,128,1024]{2,1,0:T(8,128)(2,1)} fusion(f32[128,1024]{1,0:T(8,128)S(1)} %fusion.99, bf16[128,1536]{1,0:T(8,128)(2,1)S(1)} %copy-done.6, bf16[1024,1536]{1,0:T(8,128)(2,1)S(1)} %copy-done), kind=kOutput, calls=%fused_computation.41 | convolution fusion | flops 402915328 | bytes 4325376 | tf_op jit(solution)/shard_map/dot_general | solution.py:70
  148.0 20.1 %reduce-scatter.5.cloned.1.call-done = bf16[32,1536]{1,0:T(8,128)(2,1)} async-done(((bf16[256,1536]{1,0:T(8,128)(2,1)}), bf16[32,1536]{1,0:T(8,128)(2,1)}) %reduce-scatter.5.cloned.1.call-update) | async-done | bytes 98320 | tf_op jit(solution)/shard_map/reduce_scatter | solution.py:198
  168.1 1.6 convert_multiply_fusion.2
  (34 shorter events, 0.2 us)
Async XLA Ops:
  7.2 24.0 %copy-start = (bf16[1024,1536]{1,0:T(8,128)(2,1)S(1)}, bf16[1024,1536]{1,0:T(8,128)(2,1)}, u32[]{:S(2)}) copy-start(bf16[1024,1536]{1,0:T(8,128)(2,1)} %param.19) | copy-start | bytes 9437188
  7.2 127.2 %reduce-scatter.3.cloned.1.call-start = ((), (), s32[]{:S(2)}) async-start(), calls=%async_computation.2 | async-start | bytes 3932160 | tf_op jit(solution)/shard_map/reduce_scatter | solution.py:195
  8.1 18.1 %collective-permute-start = (bf16[3,1024]{1,0:T(4,128)(2,1)S(1)}, bf16[3,1024]{1,0:T(4,128)(2,1)S(1)}, u32[]{:S(2)}, u32[]{:S(2)}) collective-permute-start(bf16[3,1024]{1,0:T(4,128)(2,1)S(1)} %get-tuple-element.12), channel_id=1, source_target_pairs={{0,1},{1,2},{2,3},{3,4},{4,5},{5,6},{6,7},{8,9},{9,10},{10,11},{11... | collective-permute-start | bytes 18440 | tf_op jit(solution)/shard_map/ppermute | solution.py:21
  10.6 15.6 %collective-permute-start.1 = (bf16[3,1024]{1,0:T(4,128)(2,1)S(1)}, bf16[3,1024]{1,0:T(4,128)(2,1)S(1)}, u32[]{:S(2)}, u32[]{:S(2)}) collective-permute-start(bf16[3,1024]{1,0:T(4,128)(2,1)S(1)} %get-tuple-element.13), channel_id=1, source_target_pairs={{1,0},{2,1},{3,2},{4,3},{5,4},{6,5},{7,6},{9,8},{10,9},{11,10},{12... | collective-permute-start | bytes 18440 | tf_op jit(solution)/shard_map/ppermute | solution.py:22
  19.7 6.6 %copy-start.8 = (bf16[1,128,1024]{2,1,0:T(8,128)(2,1)S(1)}, bf16[1,128,1024]{2,1,0:T(8,128)(2,1)}, u32[]{:S(2)}) copy-start(bf16[1,128,1024]{2,1,0:T(8,128)(2,1)} %param.14) | copy-start | bytes 786436
  19.7 8.2 %copy-start.9 = (f32[1024]{0:T(1024)S(1)}, f32[1024]{0:T(1024)}, u32[]{:S(2)}) copy-start(f32[1024]{0:T(1024)} %param.16) | copy-start | bytes 12292
  31.1 11.0 %copy-start.3 = (bf16[128,1024]{1,0:T(8,128)(2,1)}, bf16[128,1024]{1,0:T(8,128)(2,1)S(1)}, u32[]{:S(2)}) copy-start(bf16[128,1024]{1,0:T(8,128)(2,1)S(1)} %fusion.28) | copy-start | bytes 786436
  31.2 10.2 %copy-start.7 = (bf16[1,512,1536]{2,1,0:T(8,128)(2,1)S(1)}, bf16[1,512,1536]{2,1,0:T(8,128)(2,1)}, u32[]{:S(2)}) copy-start(bf16[1,512,1536]{2,1,0:T(8,128)(2,1)} %param.20) | copy-start | bytes 4718596
  31.8 6.8 %collective-permute-start.2 = (bf16[2,1536]{1,0:T(2,128)(2,1)S(1)}, bf16[2,1536]{1,0:T(2,128)(2,1)S(1)}, u32[]{:S(2)}, u32[]{:S(2)}) collective-permute-start(bf16[2,1536]{1,0:T(2,128)(2,1)S(1)} %get-tuple-element.10), channel_id=1, source_target_pairs={{0,1},{1,2},{2,3},{3,4},{4,5},{5,6},{6,7},{8,9},{9,10},{10,11},{11... | collective-permute-start | bytes 18440 | tf_op jit(solution)/shard_map/ppermute | solution.py:21
  37.0 4.3 %collective-permute-start.3 = (bf16[2,1536]{1,0:T(2,128)(2,1)S(1)}, bf16[2,1536]{1,0:T(2,128)(2,1)S(1)}, u32[]{:S(2)}, u32[]{:S(2)}) collective-permute-start(bf16[2,1536]{1,0:T(2,128)(2,1)S(1)} %get-tuple-element.11), channel_id=1, source_target_pairs={{1,0},{2,1},{3,2},{4,3},{5,4},{6,5},{7,6},{9,8},{10,9},{11,10},{12... | collective-permute-start | bytes 18440 | tf_op jit(solution)/shard_map/ppermute | solution.py:22
  42.2 1.6 copy-start.1
  75.0 9.0 %copy-start.2 = (bf16[512,1536]{1,0:T(8,128)(2,1)}, bf16[512,1536]{1,0:T(8,128)(2,1)S(1)}, u32[]{:S(2)}) copy-start(bf16[512,1536]{1,0:T(8,128)(2,1)S(1)} %fusion.10) | copy-start | bytes 4718596
  75.0 9.0 %copy-start.4 = (bf16[128,1024]{1,0:T(8,128)(2,1)S(1)}, bf16[128,1024]{1,0:T(8,128)(2,1)}, u32[]{:S(2)}) copy-start(bf16[128,1024]{1,0:T(8,128)(2,1)} %copy-done.3) | copy-start | bytes 786436
  75.6 5.1 %collective-permute-start.4 = (f32[2,1536]{1,0:T(2,128)S(1)}, f32[2,1536]{1,0:T(2,128)S(1)}, u32[]{:S(2)}, u32[]{:S(2)}) collective-permute-start(f32[2,1536]{1,0:T(2,128)S(1)} %slice.175), channel_id=1, source_target_pairs={{0,1},{1,2},{2,3},{3,4},{4,5},{5,6},{6,7},{8,9},{9,10},{10,11},{11... | collective-permute-start | bytes 36872 | tf_op jit(solution)/shard_map/ppermute | solution.py:30
  80.8 3.1 %collective-permute-start.5 = (f32[2,1536]{1,0:T(2,128)S(1)}, f32[2,1536]{1,0:T(2,128)S(1)}, u32[]{:S(2)}, u32[]{:S(2)}) collective-permute-start(f32[2,1536]{1,0:T(2,128)S(1)} %get-tuple-element.9), channel_id=1, source_target_pairs={{1,0},{2,1},{3,2},{4,3},{5,4},{6,5},{7,6},{9,8},{10,9},{11,10},{12... | collective-permute-start | bytes 36872 | tf_op jit(solution)/shard_map/ppermute | solution.py:30
  84.1 1.0 copy-start.5
  87.8 80.3 %reduce-scatter.5.cloned.1.call-start = ((), (), s32[]{:S(2)}) async-start(), calls=%async_computation.3 | async-start | bytes 884736 | tf_op jit(solution)/shard_map/reduce_scatter | solution.py:198
  145.0 1.1 copy-start.6
Sparse Core Ops, SparseCore 0:
  87.9 46.3 reduce-scatter.2
  136.6 31.4 reduce-scatter.4
where the time goes:
time: 177 us
  waiting for transfers between devices  71.7 us (41%)
  matrix products  58.1 us (33%)
  starting transfers between devices  16.3 us (9%)
  between operations  14.3 us (8%)
  other arithmetic  12.1 us (7%)
  local copies, waits for them, and re-layouts  3.97 us (2%)
    reduce_scatter x1, waiting for transfers between devices, shards(): lax.psum_scatter(proj_term.astype(jnp.bfloat16), 'dp', scatter_dimension=...  46.3 us
    reduce_scatter x1, waiting for transfers between devices, shards(): lax.psum_scatter(replica_rows, 'ctx', scatter_dimension=0, tiled=True)  20.1 us
    dot_general x3, matrix products, contract_cols(): lax.dot_general(left, right, (((1,), (1,)), ((), ())), preferred_element_...  19.7 us
    dot_general x1, matrix products, shards(): jnp.dot(hidact, ff_out_weight, preferred_element_type=jnp.float32)  10.7 us
    dot_general x1, matrix products, shards(): pre = jnp.dot(normed2, ff_in_weight, preferred_element_type=jnp.float32)  10.2 us
    ppermute x2, starting transfers between devices, extended_2(): before = lax.ppermute(last, axis, up)  7.71 us
    dot_general x1, matrix products, shards(): frame_mod = jnp.dot(utt_onehot, modul, precision=lax.Precision.HIGHEST)  6.53 us
    ppermute x2, starting transfers between devices, shifted(): return lax.ppermute(value, axis, pairs)  5.57 us
  transfers between devices with their start and end apart: 8, of which 5 were waited for; matrix products, arithmetic and copies ran while one was open for 16% of the time, Pallas kernels for 0%

commit v1 on v0

--- a/solution.py
+++ b/solution.py
@@ -1,11 +1,16 @@
+import functools
 import math
 
 import jax
 import jax.numpy as jnp
 from jax import lax
+from jax.experimental import pallas as pl
+from jax.experimental.pallas import tpu as pltpu
 from jax.sharding import PartitionSpec as P
 
-RIM = 2
+HALO = 8
+PIECES = 4
+MESH = pl.DeviceIdType.MESH
 
 
 tanh_scale = 0.7978845608028654
@@ -24,12 +29,6 @@
     return value
 
 
-def shifted(value, axis, by):
-    length = lax.axis_size(axis)
-    pairs = [(i, i + by) for i in range(length) if 0 <= i + by < length]
-    return lax.ppermute(value, axis, pairs)
-
-
 def gelu_value(inputs):
     inner = tanh_scale * (inputs + 0.044715 * inputs * inputs * inputs)
     return 0.5 * inputs * (1.0 + jnp.tanh(inner))
@@ -54,12 +53,6 @@
     return lax.rsqrt(jnp.mean(values * values, axis=-1, keepdims=True) + 1e-06)
 
 
-def split_parts(values):
-    upper_part = lax.optimization_barrier(values.astype(jnp.bfloat16))
-    lower_part = (values - upper_part.astype(jnp.float32)).astype(jnp.bfloat16)
-    return (upper_part, lower_part)
-
-
 def contract_rows(left, right):
     return lax.dot_general(
         left, right, (((0,), (0,)), ((), ())), preferred_element_type=jnp.float32
@@ -72,12 +65,228 @@
     )
 
 
-def fold_edges(window_sums, phone_local, from_lower, from_upper):
-    own_rows = window_sums[RIM : RIM + phone_local]
-    lower_rows = own_rows[:RIM] + from_lower
-    middle_rows = own_rows[RIM : phone_local - RIM]
-    upper_rows = own_rows[phone_local - RIM :] + from_upper
-    return jnp.concatenate([lower_rows, middle_rows, upper_rows], axis=0)
+def reduce_kernel(
+    dp_count,
+    ctx_count,
+    norm_factor,
+    enc_ref,
+    sums_ref,
+    proj_ref,
+    enc_grad_ref,
+    proj_grad_ref,
+    low_edge,
+    high_edge,
+    from_low,
+    from_high,
+    sums16,
+    pair_enc,
+    pair_sums,
+    terms,
+    first_in,
+    second_out,
+    second_in,
+    chip_out,
+    chip_in,
+    edge_send,
+    edge_recv,
+    pair_send,
+    pair_recv,
+    first_send,
+    first_recv,
+    second_send,
+    second_recv,
+    chip_send,
+    chip_recv,
+):
+    d = lax.axis_index("dp")
+    c = lax.axis_index("ctx")
+    core = lax.rem(c, 2)
+    chip = c // 2
+    chips = ctx_count // 2
+    pair = c + 1 - 2 * core
+    after = lax.rem(c + 1, ctx_count)
+    before = lax.rem(c + ctx_count - 1, ctx_count)
+    other = lax.rem(c + ctx_count - 1 + 2 * core, ctx_count)
+    near = jnp.where(core == 0, d + 1 - 2 * lax.rem(d, 2), lax.rem(d + dp_count // 2, dp_count))
+    far = jnp.where(core == 0, lax.rem(d + dp_count // 2, dp_count), d + 1 - 2 * lax.rem(d, 2))
+    opposite = dp_count - 1 - d
+    pieces, _, group_rows, cols = terms.shape
+    rows = group_rows // chips
+    phone_rows = enc_grad_ref.shape[0]
+    window = sums_ref.shape[0]
+
+    barrier = pltpu.get_barrier_semaphore()
+    partners = [(d, pair), (d, other), (near, c), (far, c)]
+    for i in range(1, chips):
+        partners.append((d, lax.rem(c + 2 * i, ctx_count)))
+    for partner in partners:
+        pl.semaphore_signal(barrier, inc=1, device_id=partner, device_id_type=MESH)
+
+    sums16[...] = sums_ref[...].astype(jnp.bfloat16)
+    low_edge[...] = sums_ref[:HALO, :]
+    high_edge[...] = sums_ref[window - HALO :, :]
+    pl.semaphore_wait(barrier, len(partners))
+
+    def remote(src, dst, send, recv, target):
+        return pltpu.make_async_remote_copy(
+            src_ref=src,
+            dst_ref=dst,
+            send_sem=send,
+            recv_sem=recv,
+            device_id=target,
+            device_id_type=MESH,
+        )
+
+    pair_copies = [
+        remote(sums16, pair_sums, pair_send.at[0], pair_recv.at[0], (d, pair)),
+        remote(enc_ref.at[1 - core], pair_enc, pair_send.at[1], pair_recv.at[1], (d, pair)),
+    ]
+    edge_copies = [
+        remote(low_edge, from_high, edge_send.at[0], edge_recv.at[0], (d, before)),
+        remote(high_edge, from_low, edge_send.at[1], edge_recv.at[1], (d, after)),
+    ]
+    for copy in pair_copies + edge_copies:
+        copy.start()
+    for copy in pair_copies:
+        copy.wait_recv()
+
+    own_enc = enc_ref[core]
+    their_enc = pair_enc[...]
+    first = []
+    for q in range(pieces):
+        at = slice(q * cols, (q + 1) * cols)
+        term = jnp.dot(own_enc, sums16[:, at], preferred_element_type=jnp.float32)
+        term = term + jnp.dot(their_enc, pair_sums[:, at], preferred_element_type=jnp.float32)
+        terms[q] = term.astype(jnp.bfloat16).reshape(dp_count, group_rows, cols)
+        for i, group in ((1, opposite), (0, near)):
+            copy = remote(
+                terms.at[q, group],
+                first_in.at[q, i],
+                first_send.at[q, i],
+                first_recv.at[q, i],
+                (near, c),
+            )
+            copy.start()
+            first.append((q, i, copy))
+    arrived = {(q, i): copy for q, i, copy in first}
+
+    for copy in edge_copies:
+        copy.wait_recv()
+    own = sums_ref[HALO : HALO + phone_rows, :]
+    d_cond = jnp.concatenate(
+        [
+            own[:HALO] + from_low[...],
+            own[HALO : phone_rows - HALO],
+            own[phone_rows - HALO :] + from_high[...],
+        ],
+        axis=0,
+    ).astype(jnp.bfloat16)
+    enc_grad_ref[...] = contract_cols(d_cond, proj_ref[...]).astype(jnp.bfloat16)
+
+    second = []
+    chip_copies = []
+    for q in range(pieces + 1):
+        if q < pieces:
+            arrived[q, 1].wait_recv()
+            second_out[q] = (
+                terms[q, far].astype(jnp.float32) + first_in[q, 1].astype(jnp.float32)
+            ).astype(jnp.bfloat16)
+            copy = remote(
+                second_out.at[q], second_in.at[q], second_send.at[q], second_recv.at[q], (far, c)
+            )
+            copy.start()
+            second.append(copy)
+        if q >= 1:
+            p = q - 1
+            arrived[p, 0].wait_recv()
+            second[p].wait_recv()
+            total = (
+                terms[p, d].astype(jnp.float32)
+                + first_in[p, 0].astype(jnp.float32)
+                + second_in[p].astype(jnp.float32)
+            )
+            chip_out[p] = total.reshape(chips, rows, cols).astype(jnp.bfloat16)
+            for i in range(1, chips):
+                target = lax.rem(chip + i, chips)
+                copy = remote(
+                    chip_out.at[p, target],
+                    chip_in.at[p, i],
+                    chip_send.at[p, i],
+                    chip_recv.at[p, i],
+                    (d, 2 * target + core),
+                )
+                copy.start()
+                chip_copies.append((p, copy))
+    for q in range(pieces):
+        total = chip_out[q, chip].astype(jnp.float32)
+        i = 1
+        for p, copy in chip_copies:
+            if p == q:
+                copy.wait_recv()
+                total = total + chip_in[q, i].astype(jnp.float32)
+                i += 1
+        proj_grad_ref[:, q * cols : (q + 1) * cols] = total * norm_factor
+    for copy in pair_copies + edge_copies + second:
+        copy.wait_send()
+    for _, _, copy in first:
+        copy.wait_send()
+    for _, copy in chip_copies:
+        copy.wait_send()
+
+
+def reduce_gradients(enc_window, window_sums, proj_weight, phone_local, norm_factor):
+    dp_count, ctx_count = lax.axis_size("dp"), lax.axis_size("ctx")
+    chips = ctx_count // 2
+    window, enc_width = enc_window.shape
+    width = window_sums.shape[1]
+    rows = enc_width // (dp_count * ctx_count)
+    group_rows = chips * rows
+    cols = width // PIECES
+    enc_halves = (
+        enc_window.T.reshape(dp_count * chips, 2, rows, window)
+        .transpose(1, 0, 2, 3)
+        .reshape(2, enc_width // 2, window)
+    )
+    vmem = pl.BlockSpec(memory_space=pltpu.VMEM)
+    bf16, f32, dma = jnp.bfloat16, jnp.float32, pltpu.SemaphoreType.DMA
+    return pl.pallas_call(
+        functools.partial(reduce_kernel, dp_count, ctx_count, norm_factor),
+        out_shape=(
+            jax.ShapeDtypeStruct((phone_local, enc_width), bf16),
+            jax.ShapeDtypeStruct((rows, width), f32),
+        ),
+        in_specs=[vmem] * 3,
+        out_specs=(vmem, vmem),
+        scratch_shapes=[
+            pltpu.VMEM((HALO, width), f32),
+            pltpu.VMEM((HALO, width), f32),
+            pltpu.VMEM((HALO, width), f32),
+            pltpu.VMEM((HALO, width), f32),
+            pltpu.VMEM((window, width), bf16),
+            pltpu.VMEM((enc_width // 2, window), bf16),
+            pltpu.VMEM((window, width), bf16),
+            pltpu.VMEM((PIECES, dp_count, group_rows, cols), bf16),
+            pltpu.VMEM((PIECES, 2, group_rows, cols), bf16),
+            pltpu.VMEM((PIECES, group_rows, cols), bf16),
+            pltpu.VMEM((PIECES, group_rows, cols), bf16),
+            pltpu.VMEM((PIECES, chips, rows, cols), bf16),
+            pltpu.VMEM((PIECES, chips, rows, cols), bf16),
+            dma((2,)),
+            dma((2,)),
+            dma((2,)),
+            dma((2,)),
+            dma((PIECES, 2)),
+            dma((PIECES, 2)),
+            dma((PIECES,)),
+            dma((PIECES,)),
+            dma((PIECES, chips)),
+            dma((PIECES, chips)),
+        ],
+        compiler_params=pltpu.CompilerParams(
+            collective_id=0, has_side_effects=True, vmem_limit_bytes=40 * 1024 * 1024
+        ),
+        name="reduce_gradients",
+    )(enc_halves, window_sums, proj_weight)
 
 
 def shards(
@@ -104,17 +313,18 @@
     frame_local = hidden.shape[1]
     model_width = hidden.shape[2]
     utt_ends = jnp.cumsum(utt_counts[0])
-    extended = extended_2(phone_rows, (("ctx", 0),), 3)
-    positions = ctx_index * phone_local - 3 + jnp.arange(phone_local + 6, dtype=jnp.int32)
+    window_rows = phone_local + 2 * HALO
+    extended = extended_2(phone_rows, (("ctx", 0),), HALO + 3)
+    positions = ctx_index * phone_local - HALO - 3 + jnp.arange(window_rows + 6, dtype=jnp.int32)
     segment = jnp.sum((utt_ends[None, :] <= positions[:, None]).astype(jnp.int32), axis=1)
-    centre = segment[3 : 3 + phone_local]
-    mixed = jnp.zeros((phone_local, phone_rows.shape[1]), jnp.float32)
+    centre = segment[3 : 3 + window_rows]
+    mixed = jnp.zeros((window_rows, phone_rows.shape[1]), jnp.float32)
     for offset in range(7):
-        same_utt = (segment[offset : offset + phone_local] == centre).astype(jnp.float32)
+        same_utt = (segment[offset : offset + window_rows] == centre).astype(jnp.float32)
         mixed = (
             mixed
             + conv_kernel[offset][None, :]
-            * extended[offset : offset + phone_local].astype(jnp.float32)
+            * extended[offset : offset + window_rows].astype(jnp.float32)
             * same_utt[:, None]
         )
     normed = (mixed * rms_scale(mixed) * enc_gain[None, :]).astype(jnp.bfloat16)
@@ -122,23 +332,23 @@
         jnp.bfloat16
     )
     encoded = (
-        phone_rows.astype(jnp.float32)
+        extended[3 : 3 + window_rows].astype(jnp.float32)
         + jnp.dot(inner, enc_out_weight, preferred_element_type=jnp.float32)
     ).astype(jnp.bfloat16)
     phone_dur = durations[0]
     phone_end = jnp.cumsum(phone_dur)
     phone_begin = phone_end - phone_dur
     frame_ids = ctx_index * frame_local + jnp.arange(frame_local, dtype=jnp.int32)
-    window_rows = phone_local + 2 * RIM
-    begin_padded = jnp.pad(phone_begin, RIM, constant_values=-1)
-    end_padded = jnp.pad(phone_end, RIM, constant_values=-1)
+    begin_padded = jnp.pad(phone_begin, HALO, constant_values=-1)
+    end_padded = jnp.pad(phone_end, HALO, constant_values=-1)
     begin_window = lax.dynamic_slice_in_dim(begin_padded, ctx_index * phone_local, window_rows)
     end_window = lax.dynamic_slice_in_dim(end_padded, ctx_index * phone_local, window_rows)
     onehot = (
         (frame_ids[:, None] >= begin_window[None, :]) & (frame_ids[:, None] < end_window[None, :])
     ).astype(jnp.bfloat16)
-    cond = jnp.dot(encoded, proj_weight, preferred_element_type=jnp.float32).astype(jnp.bfloat16)
-    cond_window = extended_2(cond, (("ctx", 0),), RIM)
+    cond_window = jnp.dot(encoded, proj_weight, preferred_element_type=jnp.float32).astype(
+        jnp.bfloat16
+    )
     cond_frames = jnp.dot(onehot, cond_window, preferred_element_type=jnp.float32).astype(
         jnp.bfloat16
     )
@@ -183,22 +393,10 @@
     )
     frame_gradient_rows = d_resid.astype(jnp.bfloat16)
     window_sums = contract_rows(onehot, frame_gradient_rows)
-    from_lower = shifted(window_sums[RIM + phone_local :], "ctx", 1)
-    from_upper = shifted(window_sums[:RIM], "ctx", -1)
-    d_cond = fold_edges(window_sums, phone_local, from_lower, from_upper)
-    cond_upper, cond_lower = split_parts(d_cond)
-    encoder_output_gradient = (
-        contract_cols(cond_upper, proj_weight) + contract_cols(cond_lower, proj_weight)
-    ).astype(jnp.bfloat16)
-    proj_term = contract_rows(encoded, cond_upper) + contract_rows(encoded, cond_lower)
     norm_factor = 1.0 / math.sqrt(dp_count * ctx_count * frame_local)
-    replica_rows = lax.psum_scatter(
-        proj_term.astype(jnp.bfloat16), "dp", scatter_dimension=0, tiled=True
-    )
-    grad_total = lax.psum_scatter(replica_rows, "ctx", scatter_dimension=0, tiled=True).astype(
-        jnp.float32
-    )
-    projection_weight_gradient = grad_total * norm_factor
+    encoder_output_gradient, projection_weight_gradient = reduce_gradients(
+        encoded, window_sums, proj_weight, phone_local, norm_factor
+    )
     return (
         transformer_layer_output[None],
         frame_gradient_rows[None],

time: 177 us -> 106 us (0.60)
  waiting for transfers between devices: 71.7 us -> 0.01 us
  Pallas kernels: 0 us -> 29.9 us
  between operations: 14.3 us -> 0.78 us
  starting transfers between devices: 16.3 us -> 3.65 us
  matrix products: 58.1 us -> 50.3 us
  local copies, waits for them, and re-layouts: 3.97 us -> 10.8 us
    reduce_scatter x2 -> x0, waiting for transfers between devices: 66.4 us -> none  [the longest x1 46.3 us: shards(): lax.psum_scatter(proj_term.astype(jnp.bfloat16), 'dp', scatter_dimension=...]
    pallas_call x0 -> x1, Pallas kernels: none -> 29.9 us  [reduce_gradients(): pl.pallas_call(functools.partial(reduce_kernel, dp_count, ctx_count, norm...]
    ppermute x2 -> x0, starting transfers between devices: 5.57 us -> none  [shifted(): return lax.ppermute(value, axis, pairs)]
    ppermute x2 -> x1, starting transfers between devices: 7.71 us -> 2.36 us  [extended_2(): before = lax.ppermute(last, axis, up)]
    unnamed x20 -> x16, local copies, waits for them, and re-layouts: 1.67 us -> 6.49 us
    dot_general x1, matrix products: 0.83 us -> 5.08 us  [shards(): jnp.dot(onehot, cond_window, preferred_element_type=jnp.float32)]
    dot_general x3 -> x1, matrix products: 4.24 us -> 0.58 us  [contract_rows(): lax.dot_general(left, right, (((0,), (0,)), ((), ())), preferred_element_...]
    dot_general x3 -> x1, matrix products: 19.7 us -> 16.7 us  [contract_cols(): lax.dot_general(left, right, (((1,), (1,)), ((), ())), preferred_element_...]
  transfers between devices with their start and end apart: 8 -> 2, of which waited for: 5 -> 0; matrix products, arithmetic and copies ran while one was open for 16% -> 12% of each run, Pallas kernels for 0% -> 0%
where the time goes in v1:
time: 106 us
  matrix products  50.3 us (47%)
  Pallas kernels  29.9 us (28%)
  local copies, waits for them, and re-layouts  10.8 us (10%)
  other arithmetic  10.4 us (10%)
  starting transfers between devices  3.65 us (3%)
    pallas_call x1, Pallas kernels, reduce_gradients(): pl.pallas_call(functools.partial(reduce_kernel, dp_count, ctx_count, norm...  29.9 us
    dot_general x1, matrix products, contract_cols(): lax.dot_general(left, right, (((1,), (1,)), ((), ())), preferred_element_...  16.7 us
    dot_general x1, matrix products, shards(): pre = jnp.dot(normed2, ff_in_weight, preferred_element_type=jnp.float32)  9.54 us
    dot_general x1, matrix products, shards(): jnp.dot(hidact, ff_out_weight, preferred_element_type=jnp.float32)  8.04 us
    dot_general x1, matrix products, shards(): frame_mod = jnp.dot(utt_onehot, modul, precision=lax.Precision.HIGHEST)  6.52 us
    unnamed x16, local copies, waits for them, and re-layouts  6.49 us
    dot_general x1, matrix products, shards(): jnp.dot(onehot, cond_window, preferred_element_type=jnp.float32)  5.08 us
    convert_element_type x1, other arithmetic, shards(): frame_gradient_rows = d_resid.astype(jnp.bfloat16)  4.21 us
  transfers between devices with their start and end apart: 2, of which 0 were waited for; matrix products, arithmetic and copies ran while one was open for 12% of the time, Pallas kernels for 0%

profile of v1, /device:TPU:0, one launch (start us, length us, event | category | flops | bytes accessed | tf_op | source)
XLA Modules:
  0.0 105.9 jit_solution(7990454521594377135)
XLA Ops:
  0.6 0.0 copy-start
  0.6 0.9 slice_bitcast_fusion.1
  1.6 2.4 %collective-permute-start = (bf16[11,1024]{1,0:T(8,128)(2,1)S(1)}, bf16[11,1024]{1,0:T(8,128)(2,1)S(1)}, u32[]{:S(2)}, u32[]{:S(2)}) collective-permute-start(bf16[11,1024]{1,0:T(8,128)(2,1)S(1)} %get-tuple-element.12), channel_id=1, source_target_pairs={{0,1},{1,2},{2,3},{3,4},{4,5},{5,6},{6,7},{8,9},{9,10},{10,11},{11... | collective-permute-start | bytes 67592 | tf_op jit(solution)/shard_map/ppermute | solution.py:26
  4.0 1.3 %collective-permute-start.1 = (bf16[11,1024]{1,0:T(8,128)(2,1)S(1)}, bf16[11,1024]{1,0:T(8,128)(2,1)S(1)}, u32[]{:S(2)}, u32[]{:S(2)}) collective-permute-start(bf16[11,1024]{1,0:T(8,128)(2,1)S(1)} %get-tuple-element.13), channel_id=1, source_target_pairs={{1,0},{2,1},{3,2},{4,3},{5,4},{6,5},{7,6},{9,8},{10,9},{11,10},{12... | collective-permute-start | bytes 67592 | tf_op jit(solution)/shard_map/ppermute | solution.py:27
  5.3 0.8 reduce-window.21
  6.1 0.1 convert_reduce_fusion
  6.2 0.1 compare_convert_fusion.5
  6.3 1.0 fusion.82
  7.3 1.0 reduce-window.19
  8.3 0.1 slice.96
  8.4 0.1 slice_reduce_fusion
  8.5 0.9 select_reduce_fusion
  9.4 0.8 fusion.80
  10.2 0.7 convert_bitcast_fusion
  10.8 0.1 pad_add_fusion
  10.9 0.1 multiply_sine_fusion
  11.0 0.0 copy-done
  11.0 0.4 fusion.61
  11.4 0.0 copy-start.4
  11.4 6.5 %fusion.53 = f32[512,4608]{1,0:T(8,128)} fusion(f32[4,4608]{1,0:T(4,128)S(1)} %fusion.61, s32[512]{0:T(512)S(1)} %iota_add_fusion, s32[4]{0:T(128)S(1)} %select_reduce_fusion, s32[4]{0:T(128)S(1)} %pad_add_fusion), kind=kOutput, calls=%fused_computation.73 | convolution fusion | flops 113252352 | bytes 9512992 | tf_op jit(solution)/shard_map/dot_general | solution.py:366
  17.9 0.0 copy-start.5
  17.9 0.1 pad_dynamic-slice_fusion
  18.0 0.0 collective-permute-done
  18.0 0.0 collective-permute-done.1
  18.0 0.0 copy-done.4
  18.0 0.1 pad_maximum_fusion
  18.1 1.7 %multiply_reduce_fusion.2 = (f32[144]{0:T(256)S(1)}, f32[144,1024]{1,0:T(8,128)}) fusion(f32[144]{0:T(256)S(1)} %get-tuple-element.28, bf16[150,1024]{1,0:T(8,128)(2,1)S(1)} %pad_maximum_fusion, f32[1024]{0:T(1024)S(1)} %bitcast.70, f32[144]{0:T(256)S(1)} %get-tuple-element.24, f32[1024]{0:T(1024)S(1)} %bitcast.71, f32[144]{0:T(256)S(1)} %get-tuple-element.25, ...), kind=kLoop, calls=%fused_computation.50 | loop fusion | flops 4128624 | bytes 2686912 | tf_op jit(solution)/shard_map/reduce_sum | solution.py:53
  19.8 0.0 copy-done.5
  19.8 3.4 %fusion.25 = bf16[144,1024]{1,0:T(8,128)(2,1)S(1)} fusion(bf16[1024,1024]{1,0:T(8,128)(2,1)} %param.18, bf16[1024,1024]{1,0:T(8,128)(2,1)} %param.17, f32[144,1024]{1,0:T(8,128)} %get-tuple-element.11, f32[1024]{0:T(1024)S(1)} %copy-done.5, f32[144]{0:T(256)S(1)} %add_rsqrt_fusion.1, bf16[150,1024]{1,0:T(8,128)(2,1)S(1)} %pad_maximum_fusion), kind=kOutput, calls=%fused_computation.37 | convolution fusion | flops 606191616 | bytes 5378624 | tf_op jit(solution)/shard_map/dot_general | solution.py:336
  23.2 5.1 %multiply_reduce_fusion.1 = (f32[512]{0:T(512)S(1)}, f32[512,1536]{1,0:T(8,128)}) fusion(bf16[144,1024]{1,0:T(8,128)(2,1)S(1)} %fusion.25, bf16[1024,1536]{1,0:T(8,128)(2,1)} %proj_ref.1, s32[144]{0:T(256)S(1)} %get-tuple-element.33, s32[144]{0:T(256)S(1)} %get-tuple-element.34, s32[512]{0:T(512)S(1)} %iota_add_fusion, bf16[1,512,1536]{2,1,0:T(8,128)(2,1)} %param.20), kind=kOutput, calls=%fused_computation.23 | convolution fusion | flops 684637696 | bytes 8164480 | tf_op jit(solution)/shard_map/dot_general | solution.py:352
  28.3 0.0 copy-start.2
  28.3 9.5 %fusion.19 = f32[512,2048]{1,0:T(8,128)S(1)} fusion(bf16[1536,2048]{1,0:T(8,128)(2,1)} %param.25, f32[512,4608]{1,0:T(8,128)} %fusion.53, f32[512,1536]{1,0:T(8,128)} %get-tuple-element.30, f32[512]{0:T(512)S(1)} %add_rsqrt_fusion), kind=kOutput, calls=%fused_computation.32 | convolution fusion | flops 3225157632 | bytes 19924992 | tf_op jit(solution)/shard_map/dot_general | solution.py:373
  37.8 0.0 copy-start.6
  37.8 2.1 %copy-done.6 = f32[512,2048]{1,0:T(8,128)} copy-done((f32[512,2048]{1,0:T(8,128)}, f32[512,2048]{1,0:T(8,128)S(1)}, u32[]{:S(2)}) %copy-start.6) | copy-done | bytes 4194328
  39.9 0.0 copy-done.2
  39.9 8.0 %fusion.13 = bf16[1,512,1536]{2,1,0:T(8,128)(2,1)} fusion(f32[512,1536]{1,0:T(8,128)S(1)} %copy-done.2, bf16[2048,1536]{1,0:T(8,128)(2,1)} %param.26, f32[512,4608]{1,0:T(8,128)} %fusion.53, f32[512,2048]{1,0:T(8,128)S(1)} %fusion.19), kind=kOutput, calls=%fused_computation.26 | convolution fusion | flops 3233021952 | bytes 18350080 | tf_op jit(solution)/shard_map/dot_general | solution.py:375
  47.9 16.7 %multiply_reduce_fusion = (f32[512]{0:T(512)S(1)}, f32[512,1536]{1,0:T(8,128)}) fusion(f32[512,1536]{1,0:T(8,128)} %get-tuple-element.30, f32[512,4608]{1,0:T(8,128)} %fusion.53, bf16[1536,2048]{1,0:T(8,128)(2,1)} %param.25, f32[512,2048]{1,0:T(8,128)} %copy-done.6, bf16[2048,1536]{1,0:T(8,128)(2,1)} %param.26, bf16[1,512,1536]{2,1,0:T(8,128)(2,1)} %param.27), kind=kOutput, calls=%fused_computation.22 | convolution fusion | flops 6466829824 | bytes 30935040 | tf_op jit(solution)/shard_map/dot_general | solution.py:63
  64.7 4.2 %fusion.10 = bf16[512,1536]{1,0:T(8,128)(2,1)S(1)} fusion(f32[512,1536]{1,0:T(8,128)} %get-tuple-element.32, f32[512,1536]{1,0:T(8,128)} %get-tuple-element.30, bf16[1,512,1536]{2,1,0:T(8,128)(2,1)} %param.27, f32[512]{0:T(512)S(1)} %broadcast_multiply_fusion, f32[512]{0:T(512)S(1)} %add_rsqrt_fusion), kind=kLoop, calls=%fused_computation.17 | loop fusion | flops 7077888 | bytes 9441280 | tf_op jit(solution)/shard_map/convert_element_type | solution.py:394
  68.9 0.0 copy-start.3
  68.9 1.1 %copy-done.3 = bf16[512,1536]{1,0:T(8,128)(2,1)} copy-done((bf16[512,1536]{1,0:T(8,128)(2,1)}, bf16[512,1536]{1,0:T(8,128)(2,1)S(1)}, u32[]{:S(2)}) %copy-start.3) | copy-done | bytes 1572888
  70.0 0.6 fusion.37.sums_ref
  70.6 1.0 copy.23
  71.6 1.1 %copy.24 = bf16[2,16,32,144]{3,2,1,0:T(8,128)(2,1)S(1)} copy(bf16[2,16,32,144]{3,2,0,1:T(8,128)(2,1)} %bitcast.59) | data formatting | bytes 589824 | tf_op jit(solution)/shard_map/transpose | solution.py:247
  72.7 0.0 copy-start.1
  72.7 1.9 %copy-done.1 = bf16[1024,1536]{1,0:T(8,128)(2,1)S(1)} copy-done((bf16[1024,1536]{1,0:T(8,128)(2,1)S(1)}, bf16[1024,1536]{1,0:T(8,128)(2,1)}, u32[]{:S(2)}) %copy-start.1) | copy-done | bytes 3145752
  74.6 29.9 %reduce_gradients.1 = (bf16[128,1024]{1,0:T(8,128)(2,1)S(1)}, f32[32,1536]{1,0:T(8,128)S(1)}) custom-call(bf16[2,512,144]{2,1,0:T(8,128)(2,1)S(1)} %bitcast.56, f32[144,1536]{1,0:T(8,128)S(1)} %fusion.37.sums_ref, bf16[1024,1536]{1,0:T(8,128)(2,1)S(1)} %copy-done.1), custom_call_target="tpu_custom_call" | custom-call | tf_op jit(solution)/shard_map/reduce_gradients/pallas_call | solution.py:252
  104.5 0.7 copy.27
  105.2 0.7 copy.28
  (7 shorter events, 0.1 us)
Async XLA Ops:
  0.6 10.4 %copy-start = (bf16[256,4608]{1,0:T(8,128)(2,1)S(1)}, bf16[256,4608]{1,0:T(8,128)(2,1)}, u32[]{:S(2)}) copy-start(bf16[256,4608]{1,0:T(8,128)(2,1)} %param.24) | copy-start | bytes 7077892
  1.6 16.4 %collective-permute-start = (bf16[11,1024]{1,0:T(8,128)(2,1)S(1)}, bf16[11,1024]{1,0:T(8,128)(2,1)S(1)}, u32[]{:S(2)}, u32[]{:S(2)}) collective-permute-start(bf16[11,1024]{1,0:T(8,128)(2,1)S(1)} %get-tuple-element.12), channel_id=1, source_target_pairs={{0,1},{1,2},{2,3},{3,4},{4,5},{5,6},{6,7},{8,9},{9,10},{10,11},{11... | collective-permute-start | bytes 67592 | tf_op jit(solution)/shard_map/ppermute | solution.py:26
  4.0 14.1 %collective-permute-start.1 = (bf16[11,1024]{1,0:T(8,128)(2,1)S(1)}, bf16[11,1024]{1,0:T(8,128)(2,1)S(1)}, u32[]{:S(2)}, u32[]{:S(2)}) collective-permute-start(bf16[11,1024]{1,0:T(8,128)(2,1)S(1)} %get-tuple-element.13), channel_id=1, source_target_pairs={{1,0},{2,1},{3,2},{4,3},{5,4},{6,5},{7,6},{9,8},{10,9},{11,10},{12... | collective-permute-start | bytes 67592 | tf_op jit(solution)/shard_map/ppermute | solution.py:27
  11.4 6.6 %copy-start.4 = (bf16[1,128,1024]{2,1,0:T(8,128)(2,1)S(1)}, bf16[1,128,1024]{2,1,0:T(8,128)(2,1)}, u32[]{:S(2)}) copy-start(bf16[1,128,1024]{2,1,0:T(8,128)(2,1)} %param.14) | copy-start | bytes 786436
  17.9 1.8 %copy-start.5 = (f32[1024]{0:T(1024)S(1)}, f32[1024]{0:T(1024)}, u32[]{:S(2)}) copy-start(f32[1024]{0:T(1024)} %param.16) | copy-start | bytes 12292
  28.3 11.6 %copy-start.2 = (f32[512,1536]{1,0:T(8,128)S(1)}, f32[512,1536]{1,0:T(8,128)}, u32[]{:S(2)}) copy-start(f32[512,1536]{1,0:T(8,128)} %get-tuple-element.30) | copy-start | bytes 9437188
  37.8 2.1 %copy-start.6 = (f32[512,2048]{1,0:T(8,128)}, f32[512,2048]{1,0:T(8,128)S(1)}, u32[]{:S(2)}) copy-start(f32[512,2048]{1,0:T(8,128)S(1)} %fusion.19) | copy-start | bytes 12582916
  68.9 1.1 %copy-start.3 = (bf16[512,1536]{1,0:T(8,128)(2,1)}, bf16[512,1536]{1,0:T(8,128)(2,1)S(1)}, u32[]{:S(2)}) copy-start(bf16[512,1536]{1,0:T(8,128)(2,1)S(1)} %fusion.10) | copy-start | bytes 4718596
  72.7 1.9 %copy-start.1 = (bf16[1024,1536]{1,0:T(8,128)(2,1)S(1)}, bf16[1024,1536]{1,0:T(8,128)(2,1)}, u32[]{:S(2)}) copy-start(bf16[1024,1536]{1,0:T(8,128)(2,1)} %proj_ref.1) | copy-start | bytes 9437188

commit v2 on v1

--- a/solution.py
+++ b/solution.py
@@ -10,6 +10,8 @@
 
 HALO = 8
 PIECES = 4
+NARROW = 256
+WIDE = 512
 MESH = pl.DeviceIdType.MESH
 
 
@@ -34,14 +36,6 @@
     return 0.5 * inputs * (1.0 + jnp.tanh(inner))
 
 
-def gelu_slope(inputs):
-    squared = inputs * inputs
-    hyper = jnp.tanh(tanh_scale * (inputs + 0.044715 * squared * inputs))
-    return 0.5 * (1.0 + hyper) + 0.5 * inputs * (1.0 - hyper * hyper) * tanh_scale * (
-        1.0 + 3.0 * 0.044715 * squared
-    )
-
-
 def time_embed(timestep_ids, width):
     half_width = width // 2
     frequency = jnp.exp(-math.log(10000.0) * jnp.arange(half_width, dtype=jnp.float32) / half_width)
@@ -51,12 +45,6 @@
 
 def rms_scale(values):
     return lax.rsqrt(jnp.mean(values * values, axis=-1, keepdims=True) + 1e-06)
-
-
-def contract_rows(left, right):
-    return lax.dot_general(
-        left, right, (((0,), (0,)), ((), ())), preferred_element_type=jnp.float32
-    )
 
 
 def contract_cols(left, right):
@@ -234,19 +222,14 @@
         copy.wait_send()
 
 
-def reduce_gradients(enc_window, window_sums, proj_weight, phone_local, norm_factor):
+def reduce_gradients(enc_halves, window_sums, proj_weight, phone_local, norm_factor):
     dp_count, ctx_count = lax.axis_size("dp"), lax.axis_size("ctx")
     chips = ctx_count // 2
-    window, enc_width = enc_window.shape
-    width = window_sums.shape[1]
+    enc_width = proj_weight.shape[0]
+    window, width = window_sums.shape
     rows = enc_width // (dp_count * ctx_count)
     group_rows = chips * rows
     cols = width // PIECES
-    enc_halves = (
-        enc_window.T.reshape(dp_count * chips, 2, rows, window)
-        .transpose(1, 0, 2, 3)
-        .reshape(2, enc_width // 2, window)
-    )
     vmem = pl.BlockSpec(memory_space=pltpu.VMEM)
     bf16, f32, dma = jnp.bfloat16, jnp.float32, pltpu.SemaphoreType.DMA
     return pl.pallas_call(
@@ -286,7 +269,242 @@
             collective_id=0, has_side_effects=True, vmem_limit_bytes=40 * 1024 * 1024
         ),
         name="reduce_gradients",
-    )(enc_halves, window_sums, proj_weight)
+    )(enc_halves.reshape(2, enc_width // 2, window), window_sums, proj_weight)
+
+
+def gelu_parts(inputs):
+    squared = inputs * inputs
+    hyper = jnp.tanh(tanh_scale * (inputs + 0.044715 * squared * inputs))
+    half = 0.5 * (1.0 + hyper)
+    slope = half + 0.5 * inputs * (1.0 - hyper * hyper) * tanh_scale * (
+        1.0 + 3.0 * 0.044715 * squared
+    )
+    return inputs * half, slope
+
+
+def layer_kernel(
+    ends_ref,
+    ext_ref,
+    mask_ref,
+    spans_row_ref,
+    spans_col_ref,
+    act_ref,
+    conv_ref,
+    gain_ref,
+    enc_in_hbm,
+    enc_out_hbm,
+    proj_hbm,
+    ada_hbm,
+    ff_in_hbm,
+    ff_out_hbm,
+    hidden_hbm,
+    cot_hbm,
+    out_hbm,
+    d_hidden_hbm,
+    sums_ref,
+    halves_ref,
+    enc_in,
+    enc_out,
+    proj,
+    ada,
+    ff_in,
+    ff_out,
+    hidden,
+    cot,
+    ext32,
+    modul,
+    resid,
+    normed2,
+    d_mlp,
+    hidact,
+    d_pre,
+    d_hat,
+    out_buf,
+    d_hidden,
+    sems,
+):
+    pairs = (
+        (enc_in_hbm, enc_in),
+        (enc_out_hbm, enc_out),
+        (proj_hbm, proj),
+        (ada_hbm, ada),
+        (hidden_hbm.at[0], hidden),
+        (cot_hbm.at[0], cot),
+        (ff_in_hbm, ff_in),
+        (ff_out_hbm, ff_out),
+    )
+    loads = [pltpu.make_async_copy(a, b, sems.at[i]) for i, (a, b) in enumerate(pairs)]
+    for load in loads:
+        load.start()
+    utts = ends_ref.shape[0]
+    frames, width = resid.shape
+    inner_width = hidact.shape[1]
+    window = mask_ref.shape[0]
+    groups = halves_ref.shape[1]
+
+    ext32[...] = ext_ref[...].astype(jnp.float32)
+    mixed = jnp.zeros((window, ext32.shape[1]), jnp.float32)
+    for k in range(7):
+        mixed = mixed + conv_ref[k : k + 1, :] * ext32[k : k + window, :] * mask_ref[:, k : k + 1]
+    normed = (mixed * rms_scale(mixed) * gain_ref[...]).astype(jnp.bfloat16)
+    loads[0].wait()
+    inner = gelu_value(
+        jnp.dot(normed, enc_in[...], preferred_element_type=jnp.float32)
+    ).astype(jnp.bfloat16)
+    loads[1].wait()
+    encoded = (
+        ext32[3 : 3 + window, :]
+        + jnp.dot(inner, enc_out[...], preferred_element_type=jnp.float32)
+    ).astype(jnp.bfloat16)
+    turned = encoded.astype(jnp.float32).T.reshape(groups, 2, -1, window)
+    for half in range(2):
+        halves_ref[half] = turned[:, half].astype(jnp.bfloat16)
+    loads[2].wait()
+    cond = jnp.dot(encoded, proj[...], preferred_element_type=jnp.float32).astype(jnp.bfloat16)
+    loads[3].wait()
+    modul[...] = jnp.dot(act_ref[...], ada[...], preferred_element_type=jnp.float32)
+
+    def pick(which, at, step):
+        rows = modul[:, which * width + at : which * width + at + step]
+        frame = lax.broadcasted_iota(jnp.int32, (frames, step), 0)
+        value = jnp.broadcast_to(rows[utts - 1 : utts], (frames, step))
+        for u in reversed(range(utts - 1)):
+            value = jnp.where(frame < ends_ref[u], rows[u : u + 1], value)
+        return value
+
+    frame_rows = lax.broadcasted_iota(jnp.int32, (frames, window), 0)
+    onehot = jnp.where(
+        (frame_rows >= spans_row_ref[0:1, :]) & (frame_rows < spans_row_ref[1:2, :]), 1.0, 0.0
+    ).astype(jnp.bfloat16)
+    step = NARROW
+    loads[4].wait()
+    square = jnp.zeros((frames, 1), jnp.float32)
+    for at in range(0, width, step):
+        cond_frames = jnp.dot(
+            onehot, cond[:, at : at + step], preferred_element_type=jnp.float32
+        )
+        value = hidden[:, at : at + step].astype(jnp.float32) + cond_frames
+        resid[:, at : at + step] = value
+        square = square + jnp.sum(value * value, axis=-1, keepdims=True)
+    rinv = lax.rsqrt(square * (1.0 / width) + 1e-06)
+    loads[5].wait()
+    for at in range(0, width, step):
+        cols = slice(at, at + step)
+        normed2[:, cols] = (
+            resid[:, cols] * rinv * (1.0 + pick(1, at, step)) + pick(0, at, step)
+        ).astype(jnp.bfloat16)
+        d_mlp[:, cols] = (pick(2, at, step) * cot[:, cols].astype(jnp.float32)).astype(
+            jnp.bfloat16
+        )
+    loads[6].wait()
+    loads[7].wait()
+    for at in range(0, inner_width, WIDE):
+        cols = slice(at, at + WIDE)
+        pre = jnp.dot(normed2[...], ff_in[:, cols], preferred_element_type=jnp.float32)
+        value, slope = gelu_parts(pre)
+        hidact[:, cols] = value.astype(jnp.bfloat16)
+        d_act = contract_cols(d_mlp[...], ff_out[cols, :])
+        d_pre[:, cols] = (d_act * slope).astype(jnp.bfloat16)
+    for at in range(0, width, step):
+        cols = slice(at, at + step)
+        mlp = jnp.dot(hidact[...], ff_out[:, cols], preferred_element_type=jnp.float32)
+        out_buf[:, cols] = (resid[:, cols] + pick(2, at, step) * mlp).astype(jnp.bfloat16)
+    out_store = pltpu.make_async_copy(out_buf, out_hbm.at[0], sems.at[8])
+    out_store.start()
+    inside = jnp.zeros((frames, 1), jnp.float32)
+    for at in range(0, width, step):
+        cols = slice(at, at + step)
+        value = contract_cols(d_pre[...], ff_in[cols, :]) * (1.0 + pick(1, at, step))
+        d_hat[:, cols] = value
+        inside = inside + jnp.sum(value * resid[:, cols], axis=-1, keepdims=True)
+    factor = rinv * rinv * rinv * (inside * (1.0 / width))
+    for at in range(0, width, step):
+        cols = slice(at, at + step)
+        d_hidden[:, cols] = (
+            cot[:, cols].astype(jnp.float32) + rinv * d_hat[:, cols] - resid[:, cols] * factor
+        ).astype(jnp.bfloat16)
+    d_store = pltpu.make_async_copy(d_hidden, d_hidden_hbm.at[0], sems.at[9])
+    d_store.start()
+    frame_cols = lax.broadcasted_iota(jnp.int32, (window, frames), 1)
+    turned_onehot = jnp.where(
+        (frame_cols >= spans_col_ref[:, 0:1]) & (frame_cols < spans_col_ref[:, 1:2]), 1.0, 0.0
+    ).astype(jnp.bfloat16)
+    for at in range(0, width, step):
+        cols = slice(at, at + step)
+        sums_ref[:, cols] = jnp.dot(
+            turned_onehot, d_hidden[:, cols], preferred_element_type=jnp.float32
+        )
+    out_store.wait()
+    d_store.wait()
+
+
+def layers(
+    ends,
+    extended,
+    masks,
+    spans,
+    act,
+    conv_kernel,
+    enc_gain,
+    enc_in_weight,
+    enc_out_weight,
+    proj_weight,
+    ada_weight,
+    ff_in_weight,
+    ff_out_weight,
+    hidden,
+    cotangent,
+    groups,
+):
+    frames, width = hidden.shape[1:]
+    enc_width, inner_width = conv_kernel.shape[1], ff_in_weight.shape[1]
+    window = masks.shape[0]
+    vmem = pl.BlockSpec(memory_space=pltpu.VMEM)
+    hbm = pl.BlockSpec(memory_space=pl.ANY)
+    bf16, f32 = jnp.bfloat16, jnp.float32
+    flat = (enc_in_weight, enc_out_weight, proj_weight, ada_weight, ff_in_weight, ff_out_weight)
+    return pl.pallas_call(
+        layer_kernel,
+        out_shape=(
+            jax.ShapeDtypeStruct((1, frames, width), bf16),
+            jax.ShapeDtypeStruct((1, frames, width), bf16),
+            jax.ShapeDtypeStruct((window, width), f32),
+            jax.ShapeDtypeStruct((2, groups, enc_width // (2 * groups), window), bf16),
+        ),
+        in_specs=[pl.BlockSpec(memory_space=pltpu.SMEM)] + [vmem] * 7 + [hbm] * 8,
+        out_specs=(hbm, hbm, vmem, vmem),
+        scratch_shapes=[pltpu.VMEM(a.shape, bf16) for a in flat]
+        + [
+            pltpu.VMEM((frames, width), bf16),
+            pltpu.VMEM((frames, width), bf16),
+            pltpu.VMEM(extended.shape, f32),
+            pltpu.VMEM((act.shape[0], ada_weight.shape[1]), f32),
+            pltpu.VMEM((frames, width), f32),
+            pltpu.VMEM((frames, width), bf16),
+            pltpu.VMEM((frames, width), bf16),
+            pltpu.VMEM((frames, inner_width), bf16),
+            pltpu.VMEM((frames, inner_width), bf16),
+            pltpu.VMEM((frames, width), f32),
+            pltpu.VMEM((frames, width), bf16),
+            pltpu.VMEM((frames, width), bf16),
+            pltpu.SemaphoreType.DMA((10,)),
+        ],
+        compiler_params=pltpu.CompilerParams(vmem_limit_bytes=56 * 1024 * 1024),
+        name="layers",
+    )(
+        ends,
+        extended,
+        masks,
+        spans,
+        spans.T,
+        act,
+        conv_kernel,
+        enc_gain[None],
+        *flat[:4],
+        *flat[4:],
+        hidden,
+        cotangent,
+    )
 
 
 def shards(
@@ -311,95 +529,53 @@
     phone_rows = phonemes[0]
     phone_local = phone_rows.shape[0]
     frame_local = hidden.shape[1]
-    model_width = hidden.shape[2]
     utt_ends = jnp.cumsum(utt_counts[0])
     window_rows = phone_local + 2 * HALO
     extended = extended_2(phone_rows, (("ctx", 0),), HALO + 3)
     positions = ctx_index * phone_local - HALO - 3 + jnp.arange(window_rows + 6, dtype=jnp.int32)
     segment = jnp.sum((utt_ends[None, :] <= positions[:, None]).astype(jnp.int32), axis=1)
     centre = segment[3 : 3 + window_rows]
-    mixed = jnp.zeros((window_rows, phone_rows.shape[1]), jnp.float32)
-    for offset in range(7):
-        same_utt = (segment[offset : offset + window_rows] == centre).astype(jnp.float32)
-        mixed = (
-            mixed
-            + conv_kernel[offset][None, :]
-            * extended[offset : offset + window_rows].astype(jnp.float32)
-            * same_utt[:, None]
-        )
-    normed = (mixed * rms_scale(mixed) * enc_gain[None, :]).astype(jnp.bfloat16)
-    inner = gelu_value(jnp.dot(normed, enc_in_weight, preferred_element_type=jnp.float32)).astype(
-        jnp.bfloat16
-    )
-    encoded = (
-        extended[3 : 3 + window_rows].astype(jnp.float32)
-        + jnp.dot(inner, enc_out_weight, preferred_element_type=jnp.float32)
-    ).astype(jnp.bfloat16)
+    masks = jnp.stack(
+        [segment[k : k + window_rows] == centre for k in range(7)] + [centre < 0], axis=1
+    ).astype(jnp.float32)
     phone_dur = durations[0]
     phone_end = jnp.cumsum(phone_dur)
     phone_begin = phone_end - phone_dur
-    frame_ids = ctx_index * frame_local + jnp.arange(frame_local, dtype=jnp.int32)
     begin_padded = jnp.pad(phone_begin, HALO, constant_values=-1)
     end_padded = jnp.pad(phone_end, HALO, constant_values=-1)
     begin_window = lax.dynamic_slice_in_dim(begin_padded, ctx_index * phone_local, window_rows)
     end_window = lax.dynamic_slice_in_dim(end_padded, ctx_index * phone_local, window_rows)
-    onehot = (
-        (frame_ids[:, None] >= begin_window[None, :]) & (frame_ids[:, None] < end_window[None, :])
-    ).astype(jnp.bfloat16)
-    cond_window = jnp.dot(encoded, proj_weight, preferred_element_type=jnp.float32).astype(
-        jnp.bfloat16
-    )
-    cond_frames = jnp.dot(onehot, cond_window, preferred_element_type=jnp.float32).astype(
-        jnp.bfloat16
-    )
+    spans = jnp.stack([begin_window, end_window]) - ctx_index * frame_local
     utt_marks = (
         jnp.arange(phone_dur.shape[0], dtype=jnp.int32)[None, :] < utt_ends[:, None]
     ).astype(jnp.int32)
     utt_frame_end = jnp.sum(utt_marks * phone_dur[None, :], axis=1)
-    utt_frame_begin = jnp.concatenate([jnp.zeros((1,), jnp.int32), utt_frame_end[:-1]])
-    utt_onehot = (
-        (frame_ids[:, None] >= utt_frame_begin[None, :])
-        & (frame_ids[:, None] < utt_frame_end[None, :])
-    ).astype(jnp.float32)
     act = jax.nn.silu(time_embed(timesteps[0], ada_weight.shape[0])).astype(jnp.bfloat16)
-    modul = jnp.dot(act, ada_weight, preferred_element_type=jnp.float32)
-    frame_mod = jnp.dot(utt_onehot, modul, precision=lax.Precision.HIGHEST)
-    shift = frame_mod[:, :model_width]
-    scale = frame_mod[:, model_width : 2 * model_width]
-    gate_values = frame_mod[:, 2 * model_width :]
-    residual_stream = hidden[0].astype(jnp.float32) + cond_frames.astype(jnp.float32)
-    rinv = rms_scale(residual_stream)
-    normed2 = (residual_stream * rinv * (1.0 + scale) + shift).astype(jnp.bfloat16)
-    pre = jnp.dot(normed2, ff_in_weight, preferred_element_type=jnp.float32)
-    hidact = gelu_value(pre).astype(jnp.bfloat16)
-    perceptron_output = jnp.dot(hidact, ff_out_weight, preferred_element_type=jnp.float32)
-    transformer_layer_output = (residual_stream + gate_values * perceptron_output).astype(
-        jnp.bfloat16
-    )
-    cot = cotangent[0].astype(jnp.float32)
-    d_mlp = (gate_values * cot).astype(jnp.bfloat16)
-    d_act = contract_cols(d_mlp, ff_out_weight)
-    d_pre = (d_act * gelu_slope(pre)).astype(jnp.bfloat16)
-    d_norm = contract_cols(d_pre, ff_in_weight)
-    d_hat = d_norm * (1.0 + scale)
-    d_resid = (
-        cot
-        + rinv * d_hat
-        - residual_stream
-        * rinv
-        * rinv
-        * rinv
-        * jnp.mean(d_hat * residual_stream, axis=-1, keepdims=True)
-    )
-    frame_gradient_rows = d_resid.astype(jnp.bfloat16)
-    window_sums = contract_rows(onehot, frame_gradient_rows)
+    transformer_layer_output, frame_gradient_rows, window_sums, enc_halves = layers(
+        utt_frame_end - ctx_index * frame_local,
+        extended,
+        masks,
+        spans,
+        act,
+        conv_kernel,
+        enc_gain,
+        enc_in_weight,
+        enc_out_weight,
+        proj_weight,
+        ada_weight,
+        ff_in_weight,
+        ff_out_weight,
+        hidden,
+        cotangent,
+        dp_count * ctx_count // 2,
+    )
     norm_factor = 1.0 / math.sqrt(dp_count * ctx_count * frame_local)
     encoder_output_gradient, projection_weight_gradient = reduce_gradients(
-        encoded, window_sums, proj_weight, phone_local, norm_factor
+        enc_halves, window_sums, proj_weight, phone_local, norm_factor
     )
     return (
-        transformer_layer_output[None],
-        frame_gradient_rows[None],
+        transformer_layer_output,
+        frame_gradient_rows,
         encoder_output_gradient[None],
         projection_weight_gradient,
     )

time: 106 us -> 77.7 us (0.73)
  matrix products: 50.3 us -> 0 us
  Pallas kernels: 29.9 us -> 58.7 us
  local copies, waits for them, and re-layouts: 10.8 us -> 6.24 us
  other arithmetic: 10.4 us -> 7.93 us
    dot_general x8 -> x0, matrix products: 50.3 us -> none  [the longest x1 16.7 us: contract_cols(): lax.dot_general(left, right, (((1,), (1,)), ((), ())), preferred_element_...]
    pallas_call x0 -> x1, Pallas kernels: none -> 28.8 us  [layers(): pl.pallas_call(layer_kernel, out_shape=(jax.ShapeDtypeStruct((1, frames,...]
    convert_element_type x2, other arithmetic: 4.29 us -> 0.63 us  [the longest x1 0.62 us: shards(): jax.nn.silu(time_embed(timesteps[0], ada_weight.shape[0]))]
    unnamed x16 -> x8, local copies, waits for them, and re-layouts: 6.49 us -> 3.59 us
    transpose x2 -> x0, local copies, waits for them, and re-layouts: 2.07 us -> none  [the longest x1 1.08 us: reduce_gradients(): enc_halves = enc_window.T.reshape(dp_count * chips, 2, rows, window).tran...]
    concatenate x1, other arithmetic: 0.08 us -> 1.75 us  [extended_2(): value = jnp.concatenate([before, value, after], axis=dim)]
    reduce_sum x1 -> x0, other arithmetic: 1.65 us -> none  [rms_scale(): return lax.rsqrt(jnp.mean(values * values, axis=-1, keepdims=True) + 1e-06)]
  transfers between devices with their start and end apart: 2 -> 2, of which waited for: 0 -> 0; matrix products, arithmetic and copies ran while one was open for 12% -> 10% of each run, Pallas kernels for 0% -> 0%
where the time goes in v2:
time: 77.7 us; the launch traced here: 77.3 us
  Pallas kernels  58.7 us (76%)
  other arithmetic  7.93 us (10%)
  local copies, waits for them, and re-layouts  6.24 us (8%)
  starting transfers between devices  3.65 us (5%)
    pallas_call x1, Pallas kernels, reduce_gradients(): pl.pallas_call(functools.partial(reduce_kernel, dp_count, ctx_count, norm...  29.9 us
    pallas_call x1, Pallas kernels, layers(): pl.pallas_call(layer_kernel, out_shape=(jax.ShapeDtypeStruct((1, frames,...  28.8 us
    unnamed x8, local copies, waits for them, and re-layouts  3.59 us
    ppermute x1, starting transfers between devices, extended_2(): before = lax.ppermute(last, axis, up)  2.36 us
    another operation x3, other arithmetic  1.82 us
    concatenate x1, other arithmetic, extended_2(): value = jnp.concatenate([before, value, after], axis=dim)  1.75 us
  transfers between devices with their start and end apart: 2, of which 0 were waited for; matrix products, arithmetic and copies ran while one was open for 10% of the time, Pallas kernels for 0%

profile of v2, /device:TPU:0, one launch (start us, length us, event | category | flops | bytes accessed | tf_op | source)
XLA Modules:
  0.0 77.3 jit_solution(13540431255307809033)
XLA Ops:
  0.6 0.8 %slice_bitcast_fusion.1 = (bf16[11,1024]{1,0:T(8,128)(2,1)S(1)}, bf16[11,1024]{1,0:T(8,128)(2,1)S(1)}) fusion(bf16[1,128,1024]{2,1,0:T(8,128)(2,1)} %param.14), kind=kLoop, calls=%fused_computation.3 | loop fusion | bytes 90112 | tf_op jit(solution)/shard_map/slice | solution.py:26
  1.4 2.4 %collective-permute-start = (bf16[11,1024]{1,0:T(8,128)(2,1)S(1)}, bf16[11,1024]{1,0:T(8,128)(2,1)S(1)}, u32[]{:S(2)}, u32[]{:S(2)}) collective-permute-start(bf16[11,1024]{1,0:T(8,128)(2,1)S(1)} %get-tuple-element.18), channel_id=1, source_target_pairs={{0,1},{1,2},{2,3},{3,4},{4,5},{5,6},{6,7},{8,9},{9,10},{10,11},{11... | collective-permute-start | bytes 67592 | tf_op jit(solution)/shard_map/ppermute | solution.py:28
  3.8 1.3 %collective-permute-start.1 = (bf16[11,1024]{1,0:T(8,128)(2,1)S(1)}, bf16[11,1024]{1,0:T(8,128)(2,1)S(1)}, u32[]{:S(2)}, u32[]{:S(2)}) collective-permute-start(bf16[11,1024]{1,0:T(8,128)(2,1)S(1)} %get-tuple-element.19), channel_id=1, source_target_pairs={{1,0},{2,1},{3,2},{4,3},{5,4},{6,5},{7,6},{9,8},{10,9},{11,10},{12... | collective-permute-start | bytes 67592 | tf_op jit(solution)/shard_map/ppermute | solution.py:29
  5.1 1.0 %reduce-window.20 = s32[8,128]{1,0:T(8,128)S(1)} reduce-window(s32[8,128]{1,0:T(8,128)} %bitcast.24, s32[]{:T(128)} %constant.14.clone.1), window={size=1x128 pad=0_0x127_0}, to_apply=%region_3.4 | reduce-window | flops 130048 | bytes 8196 | tf_op jit(solution)/shard_map/reduce-window.1
  6.1 0.1 slice.52
  6.2 0.1 slice_reduce_fusion
  6.3 0.8 fusion.1
  7.1 0.1 pad_dynamic-slice_fusion
  7.1 0.1 copy.35
  7.3 0.6 fusion.2.spans_col_ref
  7.9 0.8 %reduce-window.19 = s32[4,1]{0,1:T(1,128)S(1)} reduce-window(s32[4,1]{0,1:T(1,128)} %bitcast.32, s32[]{:T(128)} %constant.14.clone.1), window={size=4x1 pad=3_0x0_0}, to_apply=%region_0.0 | reduce-window | flops 12 | bytes 36 | tf_op jit(solution)/shard_map/reduce-window.6
  8.7 0.9 %select_reduce_fusion = s32[4]{0:T(128)S(1)} fusion(s32[1024]{0:T(1024)} %bitcast.26, s32[4]{0:T(128)S(1)} %bitcast.30), kind=kLoop, calls=%fused_computation.4 | loop fusion | flops 12284 | bytes 4128 | tf_op jit(solution)/shard_map/reduce_sum | solution.py:552
  9.6 0.5 broadcast_subtract_fusion.1.ends_ref
  10.1 0.7 convert_bitcast_fusion
  10.8 0.1 convert_reduce_fusion
  10.9 0.1 broadcast_compare_fusion
  10.9 0.1 multiply_sine_fusion
  11.0 0.6 fusion.act_ref
  11.8 0.7 copy.37.mask_ref
  12.5 0.7 copy.38.spans_row_ref
  13.2 0.0 collective-permute-done
  13.2 0.0 collective-permute-done.1
  13.2 1.8 %pad_maximum_fusion.ext_ref = bf16[150,1024]{1,0:T(8,128)(2,1)} fusion(bf16[11,1024]{1,0:T(8,128)(2,1)S(1)} %collective-permute-done.1, bf16[128,1024]{1,0:T(8,128)(2,1)} %bitcast.23, bf16[11,1024]{1,0:T(8,128)(2,1)S(1)} %collective-permute-done), kind=kLoop, calls=%fused_computation | loop fusion | flops 921600 | bytes 614400 | tf_op jit(solution)/shard_map/concatenate | solution.py:30
  15.0 0.0 copy-start
  15.0 28.8 %layers.1 = (bf16[1,512,1536]{2,1,0:T(8,128)(2,1)}, bf16[1,512,1536]{2,1,0:T(8,128)(2,1)}, f32[144,1536]{1,0:T(8,128)}, bf16[2,16,32,144]{3,2,1,0:T(8,128)(2,1)}) custom-call(s32[4]{0:T(128)} %broadcast_subtract_fusion.1.ends_ref, bf16[150,1024]{1,0:T(8,128)(2,1)} %pad_maximum_fusion.ext_ref, f32[144,8]{1,0:T(8,128)} %copy.37.mask_ref, ...), custom_call_target="tpu_custom_call" | custom-call | tf_op jit(solution)/shard_map/layers/pallas_call | solution.py:466
  43.8 0.0 copy-done
  43.8 0.0 copy-start.1
  43.8 1.2 %copy-done.1 = f32[144,1536]{1,0:T(8,128)S(1)} copy-done((f32[144,1536]{1,0:T(8,128)S(1)}, f32[144,1536]{1,0:T(8,128)}, u32[]{:S(2)}) %copy-start.1) | copy-done | bytes 884760
  45.0 0.0 copy-start.2
  45.0 1.0 %copy-done.2 = bf16[2,16,32,144]{3,2,1,0:T(8,128)(2,1)S(1)} copy-done((bf16[2,16,32,144]{3,2,1,0:T(8,128)(2,1)S(1)}, bf16[2,16,32,144]{3,2,1,0:T(8,128)(2,1)}, u32[]{:S(2)}) %copy-start.2) | copy-done | bytes 294936
  46.0 29.9 %reduce_gradients.1 = (bf16[128,1024]{1,0:T(8,128)(2,1)S(1)}, f32[32,1536]{1,0:T(8,128)S(1)}) custom-call(bf16[2,512,144]{2,1,0:T(8,128)(2,1)S(1)} %bitcast.21, f32[144,1536]{1,0:T(8,128)S(1)} %copy-done.1, bf16[1024,1536]{1,0:T(8,128)(2,1)S(1)} %copy-done), custom_call_target="tpu_custom_call" | custom-call | tf_op jit(solution)/shard_map/reduce_gradients/pallas_call | solution.py:235
  75.9 0.7 copy.41
  76.6 0.7 copy.42
  (15 shorter events, 0.2 us)
Async XLA Ops:
  1.4 11.8 %collective-permute-start = (bf16[11,1024]{1,0:T(8,128)(2,1)S(1)}, bf16[11,1024]{1,0:T(8,128)(2,1)S(1)}, u32[]{:S(2)}, u32[]{:S(2)}) collective-permute-start(bf16[11,1024]{1,0:T(8,128)(2,1)S(1)} %get-tuple-element.18), channel_id=1, source_target_pairs={{0,1},{1,2},{2,3},{3,4},{4,5},{5,6},{6,7},{8,9},{9,10},{10,11},{11... | collective-permute-start | bytes 67592 | tf_op jit(solution)/shard_map/ppermute | solution.py:28
  3.8 9.4 %collective-permute-start.1 = (bf16[11,1024]{1,0:T(8,128)(2,1)S(1)}, bf16[11,1024]{1,0:T(8,128)(2,1)S(1)}, u32[]{:S(2)}, u32[]{:S(2)}) collective-permute-start(bf16[11,1024]{1,0:T(8,128)(2,1)S(1)} %get-tuple-element.19), channel_id=1, source_target_pairs={{1,0},{2,1},{3,2},{4,3},{5,4},{6,5},{7,6},{9,8},{10,9},{11,10},{12... | collective-permute-start | bytes 67592 | tf_op jit(solution)/shard_map/ppermute | solution.py:29
  15.0 28.8 %copy-start = (bf16[1024,1536]{1,0:T(8,128)(2,1)S(1)}, bf16[1024,1536]{1,0:T(8,128)(2,1)}, u32[]{:S(2)}) copy-start(bf16[1024,1536]{1,0:T(8,128)(2,1)} %proj_ref.1) | copy-start | bytes 9437188
  43.8 1.2 %copy-start.1 = (f32[144,1536]{1,0:T(8,128)S(1)}, f32[144,1536]{1,0:T(8,128)}, u32[]{:S(2)}) copy-start(f32[144,1536]{1,0:T(8,128)} %get-tuple-element.13.sums_ref) | copy-start | bytes 2654212
  45.0 1.0 %copy-start.2 = (bf16[2,16,32,144]{3,2,1,0:T(8,128)(2,1)S(1)}, bf16[2,16,32,144]{3,2,1,0:T(8,128)(2,1)}, u32[]{:S(2)}) copy-start(bf16[2,16,32,144]{3,2,1,0:T(8,128)(2,1)} %get-tuple-element.12) | copy-start | bytes 884740

commit v3 on v0

v3 whole, which is shorter than its diff:
```python
import functools
import math

import jax
import jax.numpy as jnp
from jax import lax
from jax.experimental import pallas as pl
from jax.experimental.pallas import tpu as pltpu
from jax.sharding import PartitionSpec as P

HALO = 8
EDGE = 16
UTT_SLOTS = 8
PIECES = 3
WIDE = 512
MESH = pl.DeviceIdType.MESH


tanh_scale = 0.7978845608028654


def gelu_value(inputs):
    inner = tanh_scale * (inputs + 0.044715 * inputs * inputs * inputs)
    return 0.5 * inputs * (1.0 + jnp.tanh(inner))


def time_embed(timestep_ids, width):
    half_width = width // 2
    frequency = jnp.exp(-math.log(10000.0) * jnp.arange(half_width, dtype=jnp.float32) / half_width)
    angles = timestep_ids.astype(jnp.float32)[:, None] * frequency[None, :]
    return jnp.concatenate([jnp.sin(angles), jnp.cos(angles)], axis=1)


def rms_scale(values):
    return lax.rsqrt(jnp.mean(values * values, axis=-1, keepdims=True) + 1e-06)


def contract_cols(left, right):
    return lax.dot_general(
        left, right, (((1,), (1,)), ((), ())), preferred_element_type=jnp.float32
    )


def gelu_parts(inputs):
    squared = inputs * inputs
    hyper = jnp.tanh(tanh_scale * (inputs + 0.044715 * squared * inputs))
    half = 0.5 * (1.0 + hyper)
    slope = half + 0.5 * inputs * (1.0 - hyper * hyper) * tanh_scale * (
        1.0 + 3.0 * 0.044715 * squared
    )
    return inputs * half, slope


def kernel(
    dp_count,
    ctx_count,
    norm_factor,
    counts_ref,
    phone_ref,
    durations_ref,
    act_ref,
    conv_ref,
    gain_ref,
    enc_in_hbm,
    enc_out_hbm,
    proj_hbm,
    ada_hbm,
    ff_in_hbm,
    ff_out_hbm,
    hidden_hbm,
    cot_hbm,
    out_hbm,
    d_hidden_hbm,
    enc_grad_ref,
    proj_grad_ref,
    enc_in,
    enc_out,
    proj,
    ada,
    ff_in,
    ff_out,
    hidden,
    cot,
    halo_low,
    halo_high,
    ext32,
    segment,
    parts,
    resid,
    normed2,
    d_mlp,
    hidact,
    d_pre,
    out_buf,
    d_hidden,
    halves,
    sums,
    sums16,
    pair_enc,
    pair_sums,
    from_low,
    from_high,
    terms,
    first_in,
    second_out,
    second_in,
    chip_out,
    chip_in,
    load_sem,
    halo_send,
    halo_recv,
    edge_send,
    edge_recv,
    enc_send,
    enc_recv,
    pair_send,
    pair_recv,
    first_send,
    first_recv,
    second_send,
    second_recv,
    chip_send,
    chip_recv,
):
    bf16, f32 = jnp.bfloat16, jnp.float32
    d = lax.axis_index("dp")
    c = lax.axis_index("ctx")
    core = lax.rem(c, 2)
    chip = c // 2
    chips = ctx_count // 2
    pair = c + 1 - 2 * core
    after = lax.rem(c + 1, ctx_count)
    before = lax.rem(c + ctx_count - 1, ctx_count)
    other = lax.rem(c + ctx_count - 1 + 2 * core, ctx_count)
    by_low = d + 1 - 2 * lax.rem(d, 2)
    by_high = lax.rem(d + dp_count // 2, dp_count)
    near = jnp.where(core == 0, by_low, by_high)
    far = jnp.where(core == 0, by_high, by_low)
    opposite = dp_count - 1 - d
    pieces, _, group_rows, cols = terms.shape
    rows = group_rows // chips
    phones = phone_ref.shape[1]
    window = sums.shape[0]
    frames, width = resid.shape
    inner_width = hidact.shape[1]
    utts = counts_ref.shape[1]
    groups = dp_count * chips
    slots = 2 * UTT_SLOTS

    barrier = pltpu.get_barrier_semaphore()
    partners = [(d, pair), (d, other), (near, c), (far, c)]
    for i in range(1, chips):
        partners.append((d, lax.rem(c + 2 * i, ctx_count)))
    for partner in partners:
        pl.semaphore_signal(barrier, inc=1, device_id=partner, device_id_type=MESH)
    loaded = {}
    order = (
        (ada_hbm, ada),
        (cot_hbm.at[0], cot),
        (enc_in_hbm, enc_in),
        (enc_out_hbm, enc_out),
        (proj_hbm, proj),
        (hidden_hbm.at[0], hidden),
        (ff_in_hbm, ff_in),
        (ff_out_hbm, ff_out),
    )
    names = ("ada", "cot", "enc_in", "enc_out", "proj", "hidden", "ff_in", "ff_out")
    for i, (src, dst) in enumerate(order):
        loaded[names[i]] = pltpu.make_async_copy(src, dst, load_sem.at[i])
        loaded[names[i]].start()

    def remote(src, dst, send, recv, target):
        return pltpu.make_async_remote_copy(
            src_ref=src,
            dst_ref=dst,
            send_sem=send,
            recv_sem=recv,
            device_id=target,
            device_id_type=MESH,
        )

    pl.semaphore_wait(barrier, len(partners))
    halo_copies = [
        remote(
            phone_ref.at[0, phones - EDGE :], halo_low, halo_send.at[0], halo_recv.at[0], (d, after)
        ),
        remote(phone_ref.at[0, :EDGE], halo_high, halo_send.at[1], halo_recv.at[1], (d, before)),
    ]
    for copy in halo_copies:
        copy.start()

    ends = [counts_ref[0, 0]]
    for u in range(1, utts):
        ends.append(ends[u - 1] + counts_ref[0, u])
    total_phones = durations_ref.shape[1]
    spread = jnp.broadcast_to(durations_ref[...].astype(f32), (slots, total_phones)).astype(bf16)
    phone = lax.broadcasted_iota(jnp.int32, (window, total_phones), 1)
    place = c * phones - HALO + lax.broadcasted_iota(jnp.int32, (window, total_phones), 0)
    is_before = jnp.where(phone < place, 1.0, 0.0).astype(bf16)
    up_to = jnp.where(phone <= place, 1.0, 0.0).astype(bf16)
    slot = lax.broadcasted_iota(jnp.int32, (slots, total_phones), 0) % UTT_SLOTS
    low = jnp.zeros((slots, total_phones), jnp.int32)
    high = low
    for u in range(utts):
        low = jnp.where(slot == u, ends[u - 1] if u else 0, low)
        high = jnp.where(slot == u, ends[u], high)
    phone = lax.broadcasted_iota(jnp.int32, (slots, total_phones), 1)
    utt_low = contract_cols(spread, jnp.where(phone < low, 1.0, 0.0).astype(bf16))
    utt_high = contract_cols(spread, jnp.where(phone < high, 1.0, 0.0).astype(bf16))
    base = c * frames
    frame = (base + lax.broadcasted_iota(jnp.int32, (frames, slots), 0)).astype(f32)
    utt_onehot = jnp.where((frame >= utt_low[0:1, :]) & (frame < utt_high[0:1, :]), 1.0, 0.0)
    utt_onehot16 = utt_onehot.astype(bf16)
    frame = (base + lax.broadcasted_iota(jnp.int32, (frames, window), 0)).astype(f32)
    onehot = jnp.where(
        (frame >= contract_cols(spread, is_before)[0:1, :])
        & (frame < contract_cols(spread, up_to)[0:1, :]),
        1.0,
        0.0,
    ).astype(bf16)
    frame = (base + lax.broadcasted_iota(jnp.int32, (window, frames), 1)).astype(f32)
    turned_onehot = jnp.where(
        (frame >= contract_cols(is_before, spread)[:, 0:1])
        & (frame < contract_cols(up_to, spread)[:, 0:1]),
        1.0,
        0.0,
    ).astype(bf16)

    loaded["ada"].wait()
    for at in range(0, 3 * width, cols):
        modul = jnp.dot(act_ref[...], ada[:, at : at + cols], preferred_element_type=f32)
        upper = modul.astype(bf16).astype(f32)
        row = lax.broadcasted_iota(jnp.int32, (slots, cols), 0)
        parts[:, at : at + cols] = jnp.where(row < UTT_SLOTS, upper, modul - upper).astype(bf16)

    def pick(which, at):
        start = which * width + at
        return jnp.dot(utt_onehot16, parts[:, start : start + cols], preferred_element_type=f32)

    normed2[frames:, :] = parts[:, :width]
    loaded["cot"].wait()
    for at in range(0, width, cols):
        d_mlp[:, at : at + cols] = (pick(2, at) * cot[:, at : at + cols].astype(f32)).astype(bf16)

    position = c * phones - EDGE + lax.broadcasted_iota(jnp.int32, segment.shape, 0)
    number = jnp.where(position < 0, -1, 0)
    for u in range(utts):
        number = number + jnp.where(position >= ends[u], 1, 0)
    segment[...] = number
    ext32[EDGE : EDGE + phones, :] = phone_ref[0].astype(f32)
    for copy in halo_copies:
        copy.wait_recv()
    ext32[:EDGE, :] = halo_low[...].astype(f32)
    ext32[EDGE + phones :, :] = halo_high[...].astype(f32)
    shift = EDGE - HALO
    masks = [
        jnp.where(
            segment[shift + k - 3 : shift + k - 3 + window, :] == segment[shift : shift + window, :],
            1.0,
            0.0,
        )
        for k in range(7)
    ]
    lanes = segment.shape[1]
    mixed_parts = []
    for at in range(0, ext32.shape[1], lanes):
        mixed = jnp.zeros((window, lanes), f32)
        for k in range(7):
            mixed = (
                mixed
                + conv_ref[k : k + 1, at : at + lanes]
                * ext32[shift + k - 3 : shift + k - 3 + window, at : at + lanes]
                * masks[k]
            )
        mixed_parts.append(mixed)
    mixed = jnp.concatenate(mixed_parts, axis=1)
    normed = (mixed * rms_scale(mixed) * gain_ref[...]).astype(bf16)
    loaded["enc_in"].wait()
    inner = gelu_value(jnp.dot(normed, enc_in[...], preferred_element_type=f32)).astype(bf16)
    loaded["enc_out"].wait()
    encoded = (
        ext32[shift : shift + window, :]
        + jnp.dot(inner, enc_out[...], preferred_element_type=f32)
    ).astype(bf16)
    turned = encoded.astype(f32).T.reshape(groups, 2, rows, window)
    for half in range(2):
        halves[half] = turned[:, half].reshape(groups * rows, window).astype(bf16)
    enc_copy = remote(
        halves.at[1 - core], pair_enc, enc_send.at[0], enc_recv.at[0], (d, pair)
    )
    enc_copy.start()
    loaded["proj"].wait()
    cond = jnp.dot(encoded, proj[...], preferred_element_type=f32).astype(bf16)

    loaded["hidden"].wait()
    square = jnp.zeros((frames, 1), f32)
    for at in range(0, width, cols):
        value = hidden[:, at : at + cols].astype(f32) + jnp.dot(
            onehot, cond[:, at : at + cols], preferred_element_type=f32
        )
        resid[:, at : at + cols] = value
        square = square + jnp.sum(value * value, axis=-1, keepdims=True)
    square = square * (1.0 / width) + 1e-06
    rinv = lax.rsqrt(square)
    for at in range(0, width, cols):
        normed2[:frames, at : at + cols] = (
            resid[:, at : at + cols] * rinv * (1.0 + pick(1, at)) + pick(0, at)
        ).astype(bf16)
    loaded["ff_in"].wait()
    loaded["ff_out"].wait()
    inside = jnp.zeros((frames, 1), f32)
    for at in range(0, inner_width, WIDE):
        here = slice(at, at + WIDE)
        both = jnp.dot(normed2[...], ff_in[:, here], preferred_element_type=f32)
        pre = both[:frames]
        value, slope = gelu_parts(pre)
        hidact[:, here] = value.astype(bf16)
        grad = (contract_cols(d_mlp[...], ff_out[here, :]) * slope).astype(bf16)
        d_pre[:, here] = grad
        of_shift = contract_cols(grad, both[frames:].astype(bf16)) * utt_onehot
        inside = (
            inside
            + jnp.sum(grad.astype(f32) * pre, axis=-1, keepdims=True)
            - jnp.sum(of_shift, axis=-1, keepdims=True)
        )
    factor = rinv * rinv * inside * (1.0 / width)

    first = {}
    pair_copies = []

    def send_terms(q):
        at = slice(q * cols, (q + 1) * cols)
        pair_copies[q].wait_recv()
        if q == 0:
            enc_copy.wait_recv()
        term = jnp.dot(halves[core], sums16[q], preferred_element_type=f32)
        term = term + jnp.dot(pair_enc[...], pair_sums[q], preferred_element_type=f32)
        terms[q] = term.astype(bf16).reshape(dp_count, group_rows, cols)
        for i, group in ((1, opposite), (0, near)):
            first[q, i] = remote(
                terms.at[q, group],
                first_in.at[q, i],
                first_send.at[q, i],
                first_recv.at[q, i],
                (near, c),
            )
            first[q, i].start()

    for q in range(pieces):
        at = slice(q * cols, (q + 1) * cols)
        d_hat = contract_cols(d_pre[...], ff_in[at, :]) * (1.0 + pick(1, q * cols))
        d_hidden[:, at] = (
            cot[:, at].astype(f32) + rinv * d_hat - resid[:, at] * factor
        ).astype(bf16)
        piece = jnp.dot(turned_onehot, d_hidden[:, at], preferred_element_type=f32)
        sums[:, at] = piece
        sums16[q] = piece.astype(bf16)
        pair_copies.append(
            remote(sums16.at[q], pair_sums.at[q], pair_send.at[q], pair_recv.at[q], (d, pair))
        )
        pair_copies[q].start()
        if q >= 1:
            send_terms(q - 1)
    edge_copies = [
        remote(sums.at[:HALO], from_high, edge_send.at[0], edge_recv.at[0], (d, before)),
        remote(sums.at[window - HALO :], from_low, edge_send.at[1], edge_recv.at[1], (d, after)),
    ]
    for copy in edge_copies:
        copy.start()
    d_store = pltpu.make_async_copy(d_hidden, d_hidden_hbm.at[0], load_sem.at[8])
    d_store.start()
    send_terms(pieces - 1)

    second = []
    chip_copies = []
    for q in range(pieces + 1):
        if q < pieces:
            at = slice(q * cols, (q + 1) * cols)
            mlp = jnp.dot(hidact[...], ff_out[:, at], preferred_element_type=f32)
            out_buf[:, at] = (resid[:, at] + pick(2, q * cols) * mlp).astype(bf16)
            first[q, 1].wait_recv()
            second_out[q] = (terms[q, far].astype(f32) + first_in[q, 1].astype(f32)).astype(bf16)
            second.append(
                remote(
                    second_out.at[q],
                    second_in.at[q],
                    second_send.at[q],
                    second_recv.at[q],
                    (far, c),
                )
            )
            second[q].start()
        if q >= 1:
            p = q - 1
            first[p, 0].wait_recv()
            second[p].wait_recv()
            total = (
                terms[p, d].astype(f32) + first_in[p, 0].astype(f32) + second_in[p].astype(f32)
            )
            chip_out[p] = total.reshape(chips, rows, cols).astype(bf16)
            for i in range(1, chips):
                target = lax.rem(chip + i, chips)
                copy = remote(
                    chip_out.at[p, target],
                    chip_in.at[p, i],
                    chip_send.at[p, i],
                    chip_recv.at[p, i],
                    (d, 2 * target + core),
                )
                copy.start()
                chip_copies.append((p, i, copy))
        if q == pieces - 1:
            out_store = pltpu.make_async_copy(out_buf, out_hbm.at[0], load_sem.at[9])
            out_store.start()
            for copy in edge_copies:
                copy.wait_recv()
            own = sums[HALO : HALO + phones, :]
            d_cond = jnp.concatenate(
                [
                    own[:HALO] + from_low[...],
                    own[HALO : phones - HALO],
                    own[phones - HALO :] + from_high[...],
                ],
                axis=0,
            ).astype(bf16)
            enc_grad_ref[...] = contract_cols(d_cond, proj[...]).astype(bf16)
    for q in range(pieces):
        total = chip_out[q, chip].astype(f32)
        for p, i, copy in chip_copies:
            if p == q:
                copy.wait_recv()
                total = total + chip_in[q, i].astype(f32)
        proj_grad_ref[:, q * cols : (q + 1) * cols] = total * norm_factor
    for copy in halo_copies + [enc_copy] + edge_copies + pair_copies + second:
        copy.wait_send()
    for copy in first.values():
        copy.wait_send()
    for _, _, copy in chip_copies:
        copy.wait_send()
    out_store.wait()
    d_store.wait()


def shards(
    phonemes,
    conv_kernel,
    enc_gain,
    enc_in_weight,
    enc_out_weight,
    proj_weight,
    hidden,
    durations,
    utt_counts,
    timesteps,
    ada_weight,
    ff_in_weight,
    ff_out_weight,
    cotangent,
):
    dp_count, ctx_count = lax.axis_size("dp"), lax.axis_size("ctx")
    chips = ctx_count // 2
    phones, enc_width = phonemes.shape[1:]
    frames, width = hidden.shape[1:]
    inner_width = ff_in_weight.shape[1]
    window = phones + 2 * HALO
    rows = enc_width // (dp_count * ctx_count)
    group_rows = chips * rows
    cols = width // PIECES
    slots = 2 * UTT_SLOTS
    steps = jnp.pad(timesteps[0], (0, UTT_SLOTS - timesteps.shape[1]))
    act = jax.nn.silu(time_embed(jnp.concatenate([steps, steps]), ada_weight.shape[0])).astype(
        jnp.bfloat16
    )
    norm_factor = 1.0 / math.sqrt(dp_count * ctx_count * frames)
    vmem = pl.BlockSpec(memory_space=pltpu.VMEM)
    hbm = pl.BlockSpec(memory_space=pl.ANY)
    bf16, f32, dma = jnp.bfloat16, jnp.float32, pltpu.SemaphoreType.DMA
    weights = (enc_in_weight, enc_out_weight, proj_weight, ada_weight, ff_in_weight, ff_out_weight)
    out, d_hidden, enc_grad, proj_grad = pl.pallas_call(
        functools.partial(kernel, dp_count, ctx_count, norm_factor),
        out_shape=(
            jax.ShapeDtypeStruct(hidden.shape, bf16),
            jax.ShapeDtypeStruct(hidden.shape, bf16),
            jax.ShapeDtypeStruct((phones, enc_width), bf16),
            jax.ShapeDtypeStruct((rows, width), f32),
        ),
        in_specs=[pl.BlockSpec(memory_space=pltpu.SMEM)] + [vmem] * 5 + [hbm] * 8,
        out_specs=(hbm, hbm, vmem, vmem),
        scratch_shapes=[pltpu.VMEM(a.shape, bf16) for a in weights]
        + [
            pltpu.VMEM((frames, width), bf16),
            pltpu.VMEM((frames, width), bf16),
            pltpu.VMEM((EDGE, enc_width), bf16),
            pltpu.VMEM((EDGE, enc_width), bf16),
            pltpu.VMEM((phones + 2 * EDGE, enc_width), f32),
            pltpu.VMEM((phones + 2 * EDGE, 128), jnp.int32),
            pltpu.VMEM((slots, 3 * width), bf16),
            pltpu.VMEM((frames, width), f32),
            pltpu.VMEM((frames + slots, width), bf16),
            pltpu.VMEM((frames, width), bf16),
            pltpu.VMEM((frames, inner_width), bf16),
            pltpu.VMEM((frames, inner_width), bf16),
            pltpu.VMEM((frames, width), bf16),
            pltpu.VMEM((frames, width), bf16),
            pltpu.VMEM((2, enc_width // 2, window), bf16),
            pltpu.VMEM((window, width), f32),
            pltpu.VMEM((PIECES, window, cols), bf16),
            pltpu.VMEM((enc_width // 2, window), bf16),
            pltpu.VMEM((PIECES, window, cols), bf16),
            pltpu.VMEM((HALO, width), f32),
            pltpu.VMEM((HALO, width), f32),
            pltpu.VMEM((PIECES, dp_count, group_rows, cols), bf16),
            pltpu.VMEM((PIECES, 2, group_rows, cols), bf16),
            pltpu.VMEM((PIECES, group_rows, cols), bf16),
            pltpu.VMEM((PIECES, group_rows, cols), bf16),
            pltpu.VMEM((PIECES, chips, rows, cols), bf16),
            pltpu.VMEM((PIECES, chips, rows, cols), bf16),
            dma((10,)),
            dma((2,)),
            dma((2,)),
            dma((2,)),
            dma((2,)),
            dma((1,)),
            dma((1,)),
            dma((PIECES,)),
            dma((PIECES,)),
            dma((PIECES, 2)),
            dma((PIECES, 2)),
            dma((PIECES,)),
            dma((PIECES,)),
            dma((PIECES, chips)),
            dma((PIECES, chips)),
        ],
        compiler_params=pltpu.CompilerParams(
            collective_id=0, has_side_effects=True, vmem_limit_bytes=60 * 1024 * 1024
        ),
        name="layers",
    )(
        utt_counts,
        phonemes,
        durations,
        act,
        conv_kernel,
        enc_gain[None],
        *weights,
        hidden,
        cotangent,
    )
    return out, d_hidden, enc_grad[None], proj_grad


def solution(mesh):
    in_specs = (
        P("dp", "ctx", None),
        P(),
        P(),
        P(),
        P(),
        P(),
        P("dp", "ctx", None),
        P("dp", None),
        P("dp", None),
        P("dp", None),
        P(),
        P(),
        P(),
        P("dp", "ctx", None),
    )
    out_specs = (
        P("dp", "ctx", None),
        P("dp", "ctx", None),
        P("dp", "ctx", None),
        P(("dp", "ctx"), None),
    )
    return jax.shard_map(shards, mesh=mesh, in_specs=in_specs, out_specs=out_specs, check_vma=False)
```

time: 177 us -> 55.2 us (0.31)
  waiting for transfers between devices: 71.7 us -> 0 us
  matrix products: 58.1 us -> 0 us
  Pallas kernels: 0 us -> 47.5 us
  starting transfers between devices: 16.3 us -> 0 us
  between operations: 14.3 us -> 0.66 us
  other arithmetic: 12.1 us -> 0.83 us
  local copies, waits for them, and re-layouts: 3.97 us -> 5.96 us
    reduce_scatter x2 -> x0, waiting for transfers between devices: 66.4 us -> none  [the longest x1 46.3 us: shards(): lax.psum_scatter(proj_term.astype(jnp.bfloat16), 'dp', scatter_dimension=...]
    dot_general x13 -> x0, matrix products: 58.1 us -> none  [the longest x3 19.7 us: contract_cols(): lax.dot_general(left, right, (((1,), (1,)), ((), ())), preferred_element_...]
    pallas_call x0 -> x1, Pallas kernels: none -> 47.5 us  [shards(): pl.pallas_call(functools.partial(kernel, dp_count, ctx_count, norm_factor...]
    ppermute x6 -> x0, starting transfers between devices: 16 us -> none  [the longest x2 7.71 us: extended_2(): before = lax.ppermute(last, axis, up)]
    ppermute x6 -> x0, waiting for transfers between devices: 5.27 us -> none  [the longest x2 2.74 us: extended_2(): after = lax.ppermute(initial, axis, down)]
    convert_element_type x4 -> x1, other arithmetic: 4.5 us -> 0.62 us  [shards(): jax.nn.silu(time_embed(jnp.concatenate([steps, steps]), ada_weight.shape[...]
    unnamed x20 -> x10, local copies, waits for them, and re-layouts: 1.67 us -> 5.3 us
    reduce_sum x3 -> x0, other arithmetic: 2.51 us -> none  [the longest x1 1.55 us: rms_scale(): return lax.rsqrt(jnp.mean(values * values, axis=-1, keepdims=True) + 1e-06)]
  transfers between devices with their start and end apart: 8 -> 0, of which waited for: 5 -> 0; matrix products, arithmetic and copies ran while one was open for 16% -> 0% of each run, Pallas kernels for 0% -> 0%
where the time goes in v3:
time: 55.2 us; the launch traced here: 55 us
  Pallas kernels  47.5 us (86%)
  local copies, waits for them, and re-layouts  5.96 us (11%)
  other arithmetic  0.83 us (2%)
  between operations  0.66 us (1%)
    pallas_call x1, Pallas kernels, shards(): pl.pallas_call(functools.partial(kernel, dp_count, ctx_count, norm_factor...  47.5 us
    unnamed x10, local copies, waits for them, and re-layouts  5.3 us

profile of v3, /device:TPU:0, one launch (start us, length us, event | category | flops | bytes accessed | tf_op | source)
XLA Modules:
  0.0 55.0 jit_solution(986086177942054711)
XLA Ops:
  0.6 0.7 %pad.4 = s32[8]{0:T(128)S(1)} pad(s32[4]{0:T(128)} %bitcast.5, s32[]{:T(128)} %constant.3.clone.1), padding=0_4 | pad | bytes 52 | tf_op jit(solution)/shard_map/jit(_pad)/pad | solution.py:470
  1.3 0.1 add_convert_fusion
  1.4 0.1 multiply_sine_fusion
  1.5 0.6 %multiply_convert_fusion.act_ref = bf16[16,256]{1,0:T(8,128)(2,1)} fusion(f32[16,128]{1,0:T(8,128)S(1)} %get-tuple-element.13, f32[16,128]{1,0:T(8,128)S(1)} %get-tuple-element.12), kind=kLoop, calls=%fused_computation.1 | loop fusion | flops 24576 | bytes 24576 | tf_op jit(solution)/shard_map/convert_element_type | solution.py:471
  2.1 47.5 %layers.1 = (bf16[1,512,1536]{2,1,0:T(8,128)(2,1)}, bf16[1,512,1536]{2,1,0:T(8,128)(2,1)}, bf16[128,1024]{1,0:T(8,128)(2,1)}, f32[32,1536]{1,0:T(8,128)}) custom-call(s32[1,4]{1,0:T(1,128)} %counts_ref.1, bf16[1,128,1024]{2,1,0:T(8,128)(2,1)} %phone_ref.1, s32[1,1024]{1,0:T(1,128)} %durations_ref.1, bf16[16,256]{1,0:T(8,128)(2,1)} %multiply_convert_fusion.act_ref, ...), custom_call_target="tpu_custom_call" | custom-call | tf_op jit(solution)/shard_map/layers/pallas_call | solution.py:479
  49.7 0.0 copy-start
  49.7 2.8 %copy.22 = bf16[1,512,1536]{2,1,0:T(8,128)(2,1)} copy(bf16[1,512,1536]{2,1,0:T(8,128)(2,1)} %get-tuple-element.18) | data formatting | bytes 3145728
  52.5 0.0 copy-done
  52.5 0.0 copy-start.1
  52.5 0.0 copy-start.2
  52.5 1.1 %copy.23 = bf16[1,512,1536]{2,1,0:T(8,128)(2,1)} copy(bf16[1,512,1536]{2,1,0:T(8,128)(2,1)S(1)} %copy-done) | data formatting | bytes 3145728
  53.6 0.0 copy-done.1
  53.6 0.7 %copy.24 = bf16[1,128,1024]{2,1,0:T(8,128)(2,1)} copy(bf16[1,128,1024]{2,1,0:T(8,128)(2,1)S(1)} %bitcast.3) | data formatting | bytes 524288
  54.3 0.0 copy-done.2
  54.3 0.7 %copy.25 = f32[32,1536]{1,0:T(8,128)} copy(f32[32,1536]{1,0:T(8,128)S(1)} %copy-done.2) | data formatting | bytes 393216
  (1 shorter events, 0.0 us)
Async XLA Ops:
  49.7 2.8 %copy-start = (bf16[1,512,1536]{2,1,0:T(8,128)(2,1)S(1)}, bf16[1,512,1536]{2,1,0:T(8,128)(2,1)}, u32[]{:S(2)}) copy-start(bf16[1,512,1536]{2,1,0:T(8,128)(2,1)} %get-tuple-element.19) | copy-start | bytes 4718596
  52.5 1.1 %copy-start.1 = (bf16[128,1024]{1,0:T(8,128)(2,1)S(1)}, bf16[128,1024]{1,0:T(8,128)(2,1)}, u32[]{:S(2)}) copy-start(bf16[128,1024]{1,0:T(8,128)(2,1)} %get-tuple-element.10) | copy-start | bytes 786436
  52.5 1.9 %copy-start.2 = (f32[32,1536]{1,0:T(8,128)S(1)}, f32[32,1536]{1,0:T(8,128)}, u32[]{:S(2)}) copy-start(f32[32,1536]{1,0:T(8,128)} %get-tuple-element.21) | copy-start | bytes 589828

commit v4 on v3

--- a/solution.py
+++ b/solution.py
@@ -11,7 +11,7 @@
 HALO = 8
 EDGE = 16
 UTT_SLOTS = 8
-PIECES = 3
+PIECES = 6
 WIDE = 512
 MESH = pl.DeviceIdType.MESH
 
@@ -69,8 +69,8 @@
     ff_out_hbm,
     hidden_hbm,
     cot_hbm,
-    out_hbm,
-    d_hidden_hbm,
+    out_ref,
+    d_hidden_ref,
     enc_grad_ref,
     proj_grad_ref,
     enc_in,
@@ -91,8 +91,6 @@
     d_mlp,
     hidact,
     d_pre,
-    out_buf,
-    d_hidden,
     halves,
     sums,
     sums16,
@@ -179,16 +177,6 @@
             device_id_type=MESH,
         )
 
-    pl.semaphore_wait(barrier, len(partners))
-    halo_copies = [
-        remote(
-            phone_ref.at[0, phones - EDGE :], halo_low, halo_send.at[0], halo_recv.at[0], (d, after)
-        ),
-        remote(phone_ref.at[0, :EDGE], halo_high, halo_send.at[1], halo_recv.at[1], (d, before)),
-    ]
-    for copy in halo_copies:
-        copy.start()
-
     ends = [counts_ref[0, 0]]
     for u in range(1, utts):
         ends.append(ends[u - 1] + counts_ref[0, u])
@@ -226,9 +214,22 @@
         0.0,
     ).astype(bf16)
 
+    pl.semaphore_wait(barrier, len(partners))
+    halo_copies = [
+        remote(
+            phone_ref.at[0, phones - EDGE :], halo_low, halo_send.at[0], halo_recv.at[0], (d, after)
+        ),
+        remote(phone_ref.at[0, :EDGE], halo_high, halo_send.at[1], halo_recv.at[1], (d, before)),
+    ]
+    for copy in halo_copies:
+        copy.start()
+
     loaded["ada"].wait()
+    blank = jnp.zeros((UTT_SLOTS - utts, act_ref.shape[1]), f32)
+    act = act_ref[...].astype(f32)
+    act = jnp.concatenate([act, blank, act, blank], axis=0).astype(bf16)
     for at in range(0, 3 * width, cols):
-        modul = jnp.dot(act_ref[...], ada[:, at : at + cols], preferred_element_type=f32)
+        modul = jnp.dot(act, ada[:, at : at + cols], preferred_element_type=f32)
         upper = modul.astype(bf16).astype(f32)
         row = lax.broadcasted_iota(jnp.int32, (slots, cols), 0)
         parts[:, at : at + cols] = jnp.where(row < UTT_SLOTS, upper, modul - upper).astype(bf16)
@@ -349,10 +350,10 @@
     for q in range(pieces):
         at = slice(q * cols, (q + 1) * cols)
         d_hat = contract_cols(d_pre[...], ff_in[at, :]) * (1.0 + pick(1, q * cols))
-        d_hidden[:, at] = (
+        d_hidden_ref[0, :, at] = (
             cot[:, at].astype(f32) + rinv * d_hat - resid[:, at] * factor
         ).astype(bf16)
-        piece = jnp.dot(turned_onehot, d_hidden[:, at], preferred_element_type=f32)
+        piece = jnp.dot(turned_onehot, d_hidden_ref[0, :, at], preferred_element_type=f32)
         sums[:, at] = piece
         sums16[q] = piece.astype(bf16)
         pair_copies.append(
@@ -367,8 +368,6 @@
     ]
     for copy in edge_copies:
         copy.start()
-    d_store = pltpu.make_async_copy(d_hidden, d_hidden_hbm.at[0], load_sem.at[8])
-    d_store.start()
     send_terms(pieces - 1)
 
     second = []
@@ -377,7 +376,7 @@
         if q < pieces:
             at = slice(q * cols, (q + 1) * cols)
             mlp = jnp.dot(hidact[...], ff_out[:, at], preferred_element_type=f32)
-            out_buf[:, at] = (resid[:, at] + pick(2, q * cols) * mlp).astype(bf16)
+            out_ref[0, :, at] = (resid[:, at] + pick(2, q * cols) * mlp).astype(bf16)
             first[q, 1].wait_recv()
             second_out[q] = (terms[q, far].astype(f32) + first_in[q, 1].astype(f32)).astype(bf16)
             second.append(
@@ -410,8 +409,6 @@
                 copy.start()
                 chip_copies.append((p, i, copy))
         if q == pieces - 1:
-            out_store = pltpu.make_async_copy(out_buf, out_hbm.at[0], load_sem.at[9])
-            out_store.start()
             for copy in edge_copies:
                 copy.wait_recv()
             own = sums[HALO : HALO + phones, :]
@@ -437,8 +434,6 @@
         copy.wait_send()
     for _, _, copy in chip_copies:
         copy.wait_send()
-    out_store.wait()
-    d_store.wait()
 
 
 def shards(
@@ -467,10 +462,7 @@
     group_rows = chips * rows
     cols = width // PIECES
     slots = 2 * UTT_SLOTS
-    steps = jnp.pad(timesteps[0], (0, UTT_SLOTS - timesteps.shape[1]))
-    act = jax.nn.silu(time_embed(jnp.concatenate([steps, steps]), ada_weight.shape[0])).astype(
-        jnp.bfloat16
-    )
+    act = jax.nn.silu(time_embed(timesteps[0], ada_weight.shape[0])).astype(jnp.bfloat16)
     norm_factor = 1.0 / math.sqrt(dp_count * ctx_count * frames)
     vmem = pl.BlockSpec(memory_space=pltpu.VMEM)
     hbm = pl.BlockSpec(memory_space=pl.ANY)
@@ -485,7 +477,7 @@
             jax.ShapeDtypeStruct((rows, width), f32),
         ),
         in_specs=[pl.BlockSpec(memory_space=pltpu.SMEM)] + [vmem] * 5 + [hbm] * 8,
-        out_specs=(hbm, hbm, vmem, vmem),
+        out_specs=(vmem,) * 4,
         scratch_shapes=[pltpu.VMEM(a.shape, bf16) for a in weights]
         + [
             pltpu.VMEM((frames, width), bf16),
@@ -500,8 +492,6 @@
             pltpu.VMEM((frames, width), bf16),
             pltpu.VMEM((frames, inner_width), bf16),
             pltpu.VMEM((frames, inner_width), bf16),
-            pltpu.VMEM((frames, width), bf16),
-            pltpu.VMEM((frames, width), bf16),
             pltpu.VMEM((2, enc_width // 2, window), bf16),
             pltpu.VMEM((window, width), f32),
             pltpu.VMEM((PIECES, window, cols), bf16),
@@ -515,7 +505,7 @@
             pltpu.VMEM((PIECES, group_rows, cols), bf16),
             pltpu.VMEM((PIECES, chips, rows, cols), bf16),
             pltpu.VMEM((PIECES, chips, rows, cols), bf16),
-            dma((10,)),
+            dma((8,)),
             dma((2,)),
             dma((2,)),
             dma((2,)),
@@ -532,7 +522,7 @@
             dma((PIECES, chips)),
         ],
         compiler_params=pltpu.CompilerParams(
-            collective_id=0, has_side_effects=True, vmem_limit_bytes=60 * 1024 * 1024
+            collective_id=0, has_side_effects=True, vmem_limit_bytes=49 * 1024 * 1024
         ),
         name="layers",
     )(

time: 55.2 us -> 62.7 us (1.14)
  Pallas kernels: 47.5 us -> 53.6 us
  local copies, waits for them, and re-layouts: 5.96 us -> 7.4 us
    pallas_call x1, Pallas kernels: 47.5 us -> 53.6 us  [shards(): pl.pallas_call(functools.partial(kernel, dp_count, ctx_count, norm_factor...]
    unnamed x10 -> x14, local copies, waits for them, and re-layouts: 5.3 us -> 7.4 us
    pad x1 -> x0, local copies, waits for them, and re-layouts: 0.66 us -> none  [shards(): steps = jnp.pad(timesteps[0], (0, UTT_SLOTS - timesteps.shape[1]))]
where the time goes in v4:
time: 62.7 us; the launch traced here: 62.4 us
  Pallas kernels  53.6 us (85%)
  local copies, waits for them, and re-layouts  7.4 us (12%)
  other arithmetic  0.79 us (1%)
  between operations  0.67 us (1%)
    pallas_call x1, Pallas kernels, shards(): pl.pallas_call(functools.partial(kernel, dp_count, ctx_count, norm_factor...  53.6 us
    unnamed x14, local copies, waits for them, and re-layouts  7.4 us

profile of v4, /device:TPU:0, one launch (start us, length us, event | category | flops | bytes accessed | tf_op | source)
XLA Modules:
  0.0 62.4 jit_solution(15536719874917244060)
XLA Ops:
  0.6 0.7 %convert_bitcast_fusion = f32[4]{0:T(128)S(1)} fusion(s32[1,4]{1,0:T(1,128)} %param.23), kind=kLoop, calls=%fused_computation.6 | loop fusion | flops 4 | bytes 32 | tf_op jit(solution)/shard_map/convert_element_type | solution.py:30
  1.3 0.1 multiply_sine_fusion
  1.4 0.0 copy-start
  1.4 0.9 %copy-done = bf16[1,128,1024]{2,1,0:T(8,128)(2,1)S(1)} copy-done((bf16[1,128,1024]{2,1,0:T(8,128)(2,1)S(1)}, bf16[1,128,1024]{2,1,0:T(8,128)(2,1)}, u32[]{:S(2)}) %copy-start) | copy-done | bytes 262168
  2.4 0.0 copy-start.1
  2.4 0.8 %copy-done.1 = f32[7,1024]{1,0:T(8,128)S(1)} copy-done((f32[7,1024]{1,0:T(8,128)S(1)}, f32[7,1024]{1,0:T(8,128)}, u32[]{:S(2)}) %copy-start.1) | copy-done | bytes 28696
  3.2 0.0 copy-start.2
  3.2 0.7 %copy-done.2 = s32[1,1024]{1,0:T(1,128)S(1)} copy-done((s32[1,1024]{1,0:T(1,128)S(1)}, s32[1,1024]{1,0:T(1,128)}, u32[]{:S(2)}) %copy-start.2) | copy-done | bytes 4120
  3.8 0.0 copy-start.3
  3.8 0.7 %copy-done.3 = f32[1024]{0:T(1024)S(1)} copy-done((f32[1024]{0:T(1024)S(1)}, f32[1024]{0:T(1024)}, u32[]{:S(2)}) %copy-start.3) | copy-done | bytes 4120
  4.5 0.0 copy-start.4
  4.5 0.7 %copy-done.4 = s32[1,4]{1,0:T(1,128)S(1)} copy-done((s32[1,4]{1,0:T(1,128)S(1)}, s32[1,4]{1,0:T(1,128)}, u32[]{:S(2)}) %copy-start.4) | copy-done | bytes 40
  5.2 53.6 %layers.1 = (bf16[1,512,1536]{2,1,0:T(8,128)(2,1)S(1)}, bf16[1,512,1536]{2,1,0:T(8,128)(2,1)S(1)}, bf16[128,1024]{1,0:T(8,128)(2,1)S(1)}, f32[32,1536]{1,0:T(8,128)S(1)}) custom-call(s32[1,4]{1,0:T(1,128)S(1)} %copy-done.4, bf16[1,128,1024]{2,1,0:T(8,128)(2,1)S(1)} %copy-done, s32[1,1024]{1,0:T(1,128)S(1)} %copy-done.2, bf16[4,256]{1,0:T(4,128)(2,1)S(1)} %fusion.act_ref, ...), custom_call_target="tpu_custom_call" | custom-call | tf_op jit(solution)/shard_map/layers/pallas_call | solution.py:471
  58.8 1.1 %copy.22 = bf16[1,512,1536]{2,1,0:T(8,128)(2,1)} copy(bf16[1,512,1536]{2,1,0:T(8,128)(2,1)S(1)} %get-tuple-element.18) | data formatting | bytes 3145728
  59.9 1.1 %copy.23 = bf16[1,512,1536]{2,1,0:T(8,128)(2,1)} copy(bf16[1,512,1536]{2,1,0:T(8,128)(2,1)S(1)} %get-tuple-element.19) | data formatting | bytes 3145728
  61.0 0.7 %copy.24 = bf16[1,128,1024]{2,1,0:T(8,128)(2,1)} copy(bf16[1,128,1024]{2,1,0:T(8,128)(2,1)S(1)} %bitcast.4) | data formatting | bytes 524288
  61.8 0.7 %copy.25 = f32[32,1536]{1,0:T(8,128)} copy(f32[32,1536]{1,0:T(8,128)S(1)} %get-tuple-element.21) | data formatting | bytes 393216
  (2 shorter events, 0.0 us)
Async XLA Ops:
  1.4 1.0 %copy-start = (bf16[1,128,1024]{2,1,0:T(8,128)(2,1)S(1)}, bf16[1,128,1024]{2,1,0:T(8,128)(2,1)}, u32[]{:S(2)}) copy-start(bf16[1,128,1024]{2,1,0:T(8,128)(2,1)} %phone_ref.1) | copy-start | bytes 786436
  2.4 0.8 %copy-start.1 = (f32[7,1024]{1,0:T(8,128)S(1)}, f32[7,1024]{1,0:T(8,128)}, u32[]{:S(2)}) copy-start(f32[7,1024]{1,0:T(8,128)} %conv_ref.1) | copy-start | bytes 86020
  3.2 0.7 %copy-start.2 = (s32[1,1024]{1,0:T(1,128)S(1)}, s32[1,1024]{1,0:T(1,128)}, u32[]{:S(2)}) copy-start(s32[1,1024]{1,0:T(1,128)} %durations_ref.1) | copy-start | bytes 12292
  3.8 0.7 %copy-start.3 = (f32[1024]{0:T(1024)S(1)}, f32[1024]{0:T(1024)}, u32[]{:S(2)}) copy-start(f32[1024]{0:T(1024)} %param.16) | copy-start | bytes 12292
  4.5 0.7 %copy-start.4 = (s32[1,4]{1,0:T(1,128)S(1)}, s32[1,4]{1,0:T(1,128)}, u32[]{:S(2)}) copy-start(s32[1,4]{1,0:T(1,128)} %counts_ref.1) | copy-start | bytes 52
